TPU v7x, 32 devices: a whole 2x2x4 slice. The times are simulated.
32 devices in a mesh: fsdp: 4 (over z), ctx: 4 (over y, x), tp: 2 (over core).
Axes of the slice: x: 2, y: 2, z: 4, core: 2. Of those that a mesh axis runs over, the one named last changes fastest.
Arguments:
- tokens: bfloat16 [4, 4096, 1024], P('fsdp', 'ctx'), may hold values from -6 to 6
- doc_ids: int32 [4, 4096], P('fsdp', 'ctx'), may hold values from 0 to 2, as said below
- prenorm: bfloat16 [1024], P('fsdp'), may hold values from 0.5 to 1.5
- w_query: bfloat16 [1024, 512], P('fsdp', 'tp'), may hold values from -0.1875 to 0.1875
- w_key: bfloat16 [1024, 512], P('fsdp', 'tp'), may hold values from -0.1875 to 0.1875
- w_value: bfloat16 [1024, 1024], P('fsdp', 'tp'), may hold values from -0.1875 to 0.1875
- w_outgate: bfloat16 [1024, 1024], P('fsdp', 'tp'), may hold values from -0.1875 to 0.1875
- w_lowrank: bfloat16 [1024, 16], P('fsdp'), may hold values from -0.1875 to 0.1875
- w_decay: bfloat16 [16, 512], P(None, 'tp'), may hold values from -1.5 to 1.5
- decay_bias: bfloat16 [512], P('tp'), may hold values from -2 to 5
- headnorm: bfloat16 [256], replicated, may hold values from 0.5 to 1.5
- w_output: bfloat16 [1024, 1024], P('tp', 'fsdp'), may hold values from -0.375 to 0.375
- postnorm: bfloat16 [1024], P('fsdp'), may hold values from 0.5 to 1.5
- w_gate: bfloat16 [1024, 2816], P('fsdp', 'tp'), may hold values from -0.1875 to 0.1875
- w_up: bfloat16 [1024, 2816], P('fsdp', 'tp'), may hold values from -0.1875 to 0.1875
- w_down: bfloat16 [2816, 1024], P('tp', 'fsdp'), may hold values from -0.21875 to 0.21875
- cotangent: bfloat16 [4, 4096, 1024], P('fsdp', 'ctx'), may hold values from -6 to 6
Outputs:
- block_out: bfloat16 [4, 4096, 1024], P('fsdp', 'ctx')
- grad_tokens: bfloat16 [4, 4096, 1024], P('fsdp', 'ctx')
- grad_prenorm: float32 [1024], P('fsdp')
- grad_query: float32 [1024, 512], P('fsdp', 'tp')
- grad_key: float32 [1024, 512], P('fsdp', 'tp')
- grad_value: float32 [1024, 1024], P('fsdp', 'tp')
- grad_outgate: float32 [1024, 1024], P('fsdp', 'tp')
- grad_lowrank: float32 [1024, 16], P('fsdp')
- grad_decay: float32 [16, 512], P(None, 'tp')
- grad_bias: float32 [512], P('tp')
- grad_headnorm: float32 [256], replicated
- grad_output: float32 [1024, 1024], P('tp', 'fsdp')
- grad_postnorm: float32 [1024], P('fsdp')
- grad_gate: float32 [1024, 2816], P('fsdp', 'tp')
- grad_up: float32 [1024, 2816], P('fsdp', 'tp')
- grad_down: float32 [2816, 1024], P('tp', 'fsdp')
Inputs may be any that keep to these rules, and one draw needn't show every extreme that they name: `doc_ids`: every sequence holds three documents numbered 0, 1, 2 in order. Document 0 begins the sequence and ends within its first 1024 tokens; document 2 begins within its last 1024 tokens and ends it; documents 0 and 2 have 200 tokens or more.
All inputs are finite; a program needn't handle non-finite values.
Results may differ from a plain program's by a relative error of at most 0.029.
Values may be sent and summed in bfloat16 or wider, within the bound.
A program may use at most 128 MiB of HBM per device.

v0:
```python
import jax
import jax.numpy as jnp
from jax import lax
from jax.sharding import PartitionSpec as P

KH = 128
VH = 256
BLOCK = 64


EPSILON = 1e-06
HEAD_FLOOR = 1.0
NORMALIZER = 16.0


def shifted(value, axis, steps):
    count = lax.axis_size(axis)
    initial, last = (max(0, -steps), min(count, count - steps))
    return lax.ppermute(value, axis, [(source, source + steps) for source in range(initial, last)])


def entering(part, axis, combine, identity):
    place = lax.axis_index(axis)
    gathered = jax.tree.map(lambda a: lax.all_gather(a, axis), part)
    state = jax.tree.map(lambda a, e: jnp.zeros_like(a) + jnp.asarray(e, a.dtype), part, identity)

    def entering_one(turn, state):
        return combine(
            state, jax.tree.map(lambda a: lax.dynamic_index_in_dim(a, turn, 0, False), gathered)
        )

    return lax.fori_loop(0, place, entering_one, state)


def prefix(array, axis, join, neutral):
    count = lax.axis_size(axis)
    place = lax.axis_index(axis)
    ahead = count - 1 - place
    gathered = jax.tree.map(
        lambda a, kind: lax.all_gather(a.astype(kind), axis),
        array,
        jax.tree.map(lambda a: jnp.bfloat16 if a.dtype == jnp.float32 else a.dtype, array),
    )
    state = jax.tree.map(lambda a, e: jnp.zeros_like(a) + jnp.asarray(e, a.dtype), array, neutral)

    def prefix_one(turn, state):
        source = count - 1 - turn
        return join(
            state,
            jax.tree.map(
                lambda a, own: lax.dynamic_index_in_dim(a, source, 0, False).astype(own.dtype),
                gathered,
                array,
            ),
        )

    return lax.fori_loop(0, ahead, prefix_one, state)


def block_step(carry, blocks):
    running, prev_ids = carry
    query_rows, key_rows, value_rows, decay_rows, id_rows = blocks
    total = jnp.cumsum(decay_rows, axis=2)
    block_len = id_rows.shape[1]
    later = lax.broadcasted_iota(jnp.int32, (block_len, block_len), 0)
    earlier = lax.broadcasted_iota(jnp.int32, (block_len, block_len), 1)
    linked = (id_rows[:, :, None] == id_rows[:, None, :]) & (later >= earlier)[None, :, :]
    anchor = total[:, :, block_len // 2 : block_len // 2 + 1, :]
    query_scaled = query_rows * jnp.exp(total - anchor)
    key_scaled = key_rows * jnp.exp(anchor - total)
    raw = jnp.einsum("bhtk,bhsk->bhts", query_scaled, key_scaled, precision=lax.Precision.HIGHEST)
    scores = jnp.where(linked[:, None, :, :], raw, 0.0)
    inner = jnp.einsum("bhts,bhsv->bhtv", scores, value_rows, precision=lax.Precision.HIGHEST)
    alive = (id_rows == prev_ids[:, None]).astype(jnp.float32)
    reach = query_rows * jnp.exp(total) * alive[:, None, :, None]
    carried = jnp.einsum("bhtk,bhkv->bhtv", reach, running, precision=lax.Precision.HIGHEST)
    last_ids = id_rows[:, -1]
    keep = (id_rows == last_ids[:, None]).astype(jnp.float32)
    tail = jnp.exp(total[:, :, -1:, :] - total) * keep[:, None, :, None]
    fresh = jnp.einsum(
        "bhsk,bhsv->bhkv", key_rows * tail, value_rows, precision=lax.Precision.HIGHEST
    )
    survive = (last_ids == prev_ids).astype(jnp.float32)
    running = (
        survive[:, None, None, None] * jnp.exp(total[:, :, -1, :])[:, :, :, None] * running + fresh
    )
    return ((running, last_ids), inner + carried)


def run_blocks(query_all, key_all, value_all, decay_all, doc_rows, running, prev_ids):
    seq_count, head_count, length_all, key_size = query_all.shape
    value_size = value_all.shape[-1]
    count_blocks = length_all // BLOCK

    def split_rows(array):
        return jnp.moveaxis(
            array.reshape(seq_count, head_count, count_blocks, BLOCK, array.shape[-1]), 2, 0
        )

    id_blocks = jnp.moveaxis(doc_rows.reshape(seq_count, count_blocks, BLOCK), 1, 0)
    _, outputs = lax.scan(
        jax.checkpoint(block_step),
        (running, prev_ids),
        (
            split_rows(query_all),
            split_rows(key_all),
            split_rows(value_all),
            split_rows(decay_all),
            id_blocks,
        ),
    )
    return jnp.moveaxis(outputs, 0, 2).reshape(seq_count, head_count, length_all, value_size)


def project(left, matrix):
    return jnp.einsum("bpd,de->bpe", left, matrix, preferred_element_type=jnp.float32)


def project_back(grad_rows, matrix):
    return jnp.einsum("bpe,de->bpd", grad_rows, matrix, preferred_element_type=jnp.float32)


def weight_grad(left, grad_rows):
    return jnp.einsum("bpd,bpe->de", left, grad_rows, preferred_element_type=jnp.float32)


def rms_scale(rows):
    return lax.rsqrt(jnp.mean(rows * rows, axis=-1, keepdims=True) + EPSILON)


def head_scale_of(rows):
    return lax.rsqrt(jnp.mean(rows * rows, axis=-1, keepdims=True) + HEAD_FLOOR)


def norm_back(grad_normed, rows, scale, gain):
    inner_term = gain * grad_normed
    return scale * (
        inner_term - rows * scale * scale * jnp.mean(inner_term * rows, axis=-1, keepdims=True)
    )


def to_heads(array, size):
    shaped = array.reshape(array.shape[0], array.shape[1], -1, size)
    return jnp.transpose(shaped, (0, 2, 1, 3)).astype(jnp.float32)


def from_heads(array):
    moved = jnp.transpose(array, (0, 2, 1, 3))
    return moved.reshape(moved.shape[0], moved.shape[1], -1)


def compose_pair(earlier, later):
    return (earlier[0] * later[0], later[0][..., None] * earlier[1] + later[1])


def body(
    tokens,
    doc_ids,
    prenorm,
    w_query,
    w_key,
    w_value,
    w_outgate,
    w_lowrank,
    w_decay,
    decay_bias,
    headnorm,
    w_output,
    postnorm,
    w_gate,
    w_up,
    w_down,
    cotangent,
):
    (
        gain_one,
        mat_query,
        mat_key,
        mat_value,
        mat_outgate,
        mat_lowrank,
        mat_output,
        gain_two,
        mat_gate,
        mat_up,
        mat_down,
    ) = (
        lax.all_gather(prenorm, "fsdp", axis=0, tiled=True),
        lax.all_gather(w_query, "fsdp", axis=0, tiled=True),
        lax.all_gather(w_key, "fsdp", axis=0, tiled=True),
        lax.all_gather(w_value, "fsdp", axis=0, tiled=True),
        lax.all_gather(w_outgate, "fsdp", axis=0, tiled=True),
        lax.all_gather(w_lowrank, "fsdp", axis=0, tiled=True),
        lax.all_gather(w_output, "fsdp", axis=1, tiled=True),
        lax.all_gather(postnorm, "fsdp", axis=0, tiled=True),
        lax.all_gather(w_gate, "fsdp", axis=0, tiled=True),
        lax.all_gather(w_up, "fsdp", axis=0, tiled=True),
        lax.all_gather(w_down, "fsdp", axis=1, tiled=True),
    )
    seq_count, piece_len, model_width = tokens.shape
    local_heads = w_query.shape[1] // KH
    gain_first = gain_one.astype(jnp.float32)
    gain_second = gain_two.astype(jnp.float32)
    gain_head = headnorm.astype(jnp.float32)
    resid_in = tokens.astype(jnp.float32)
    scale_one = rms_scale(resid_in)
    normed_one = (resid_in * scale_one * gain_first).astype(jnp.bfloat16)
    query_lin = project(normed_one, mat_query).astype(jnp.bfloat16)
    key_lin = project(normed_one, mat_key).astype(jnp.bfloat16)
    value_lin = project(normed_one, mat_value).astype(jnp.bfloat16)
    gate_pre = project(normed_one, mat_outgate)
    rank_act = project(normed_one, mat_lowrank).astype(jnp.bfloat16)
    decay_logit = project(rank_act, w_decay) + decay_bias.astype(jnp.float32)
    log_decay = jax.nn.log_sigmoid(decay_logit) / NORMALIZER
    query_heads = to_heads(query_lin, KH)
    key_heads = to_heads(key_lin, KH)
    value_heads = to_heads(value_lin, VH)
    decay_heads = to_heads(log_decay, KH)
    last_ids = doc_ids[:, -1]
    prev_ids = shifted(last_ids, "ctx", 1)
    link = (last_ids == prev_ids).astype(jnp.float32)

    def ending(key_part, value_part, decay_part):
        total = jnp.cumsum(decay_part, axis=2)
        keep = (doc_ids == last_ids[:, None]).astype(jnp.float32)
        tail = jnp.exp(total[:, :, -1:, :] - total) * keep[:, None, :, None]
        fresh = jnp.einsum(
            "bhsk,bhsv->bhkv", key_part * tail, value_part, precision=lax.Precision.HIGHEST
        )
        return (fresh, jnp.exp(total[:, :, -1, :]))

    (fresh_state, decay_total), ending_back = jax.vjp(ending, key_heads, value_heads, decay_heads)
    carry_decay = decay_total * link[:, None, None]
    identity_pair = (jnp.ones_like(carry_decay), jnp.zeros_like(fresh_state))
    _, incoming = entering((carry_decay, fresh_state), "ctx", compose_pair, identity_pair)

    def mixer_local(query_part, key_part, value_part, decay_part, start_state):
        return run_blocks(
            query_part * KH ** (-0.5),
            key_part,
            value_part,
            decay_part,
            doc_ids,
            start_state,
            prev_ids,
        )

    mixed, mixer_back = jax.vjp(
        mixer_local, query_heads, key_heads, value_heads, decay_heads, incoming
    )
    mix_rows = jnp.transpose(mixed, (0, 2, 1, 3))
    head_scale = head_scale_of(mix_rows)
    unit_rows = mix_rows * head_scale
    gate_rows = gate_pre.reshape(seq_count, piece_len, local_heads, VH)
    gate_sig = jax.nn.sigmoid(gate_rows)
    swish = gate_rows * gate_sig
    gated = (
        (unit_rows * gain_head * swish)
        .astype(jnp.bfloat16)
        .reshape(seq_count, piece_len, local_heads * VH)
    )
    attn_full = lax.psum(project(gated, mat_output), "tp")
    resid_mid = resid_in + attn_full
    scale_two = rms_scale(resid_mid)
    normed_two = (resid_mid * scale_two * gain_second).astype(jnp.bfloat16)
    gate_act = project(normed_two, mat_gate)
    up_act = project(normed_two, mat_up)
    ffn_sig = jax.nn.sigmoid(gate_act)
    silu_act = gate_act * ffn_sig
    hidden = (silu_act * up_act).astype(jnp.bfloat16)
    ffn_full = lax.psum(project(hidden, mat_down).astype(jnp.bfloat16), "tp").astype(jnp.float32)
    block_out = (resid_mid + ffn_full).astype(jnp.bfloat16)
    grad_down = weight_grad(hidden, cotangent)
    grad_hidden = project_back(cotangent, mat_down)
    grad_gate_act = (grad_hidden * up_act * ffn_sig * (1.0 + gate_act * (1.0 - ffn_sig))).astype(
        jnp.bfloat16
    )
    grad_up_act = (grad_hidden * silu_act).astype(jnp.bfloat16)
    grad_gate = weight_grad(normed_two, grad_gate_act)
    grad_up = weight_grad(normed_two, grad_up_act)
    back_two = project_back(grad_gate_act, mat_gate) + project_back(grad_up_act, mat_up)
    norm_two_grad = lax.psum(back_two.astype(jnp.bfloat16), "tp").astype(jnp.float32)
    grad_postnorm = jnp.sum(norm_two_grad * resid_mid * scale_two, axis=(0, 1))
    grad_mid = cotangent.astype(jnp.float32) + norm_back(
        norm_two_grad, resid_mid, scale_two, gain_second
    )
    grad_attn = grad_mid.astype(jnp.bfloat16)
    grad_output = weight_grad(gated, grad_attn)
    grad_gated = project_back(grad_attn, mat_output).reshape(seq_count, piece_len, local_heads, VH)
    headnorm_part = jnp.sum(grad_gated * unit_rows * swish, axis=(0, 1, 2))
    grad_swish = grad_gated * unit_rows * gain_head
    grad_gate_rows = (grad_swish * gate_sig * (1.0 + gate_rows * (1.0 - gate_sig))).astype(
        jnp.bfloat16
    )
    grad_gate_rows = grad_gate_rows.reshape(seq_count, piece_len, local_heads * VH)
    grad_unit = grad_gated * gain_head * swish
    grad_mix_rows = head_scale * (
        grad_unit - unit_rows * jnp.mean(grad_unit * unit_rows, axis=-1, keepdims=True)
    )
    grad_mixed = jnp.transpose(grad_mix_rows, (0, 2, 1, 3))
    mix_query, mix_key, mix_value, mix_decay, grad_incoming = mixer_back(grad_mixed)
    _, grad_ending = prefix((carry_decay, grad_incoming), "ctx", compose_pair, identity_pair)
    grad_decay_total = link[:, None, None] * jnp.sum(grad_ending * incoming, axis=-1)
    end_key, end_value, end_decay = ending_back((grad_ending, grad_decay_total))
    grad_query_rows = from_heads(mix_query).astype(jnp.bfloat16)
    grad_key_rows = from_heads(mix_key + end_key).astype(jnp.bfloat16)
    grad_value_rows = from_heads(mix_value + end_value).astype(jnp.bfloat16)
    grad_log_decay = from_heads(mix_decay + end_decay)
    grad_logit = (grad_log_decay * jax.nn.sigmoid(-decay_logit) / NORMALIZER).astype(jnp.bfloat16)
    grad_decay = jnp.einsum("bpr,bpk->rk", rank_act, grad_logit, preferred_element_type=jnp.float32)
    grad_bias = jnp.sum(grad_logit.astype(jnp.float32), axis=(0, 1))
    rank_part = jnp.einsum("bpk,rk->bpr", grad_logit, w_decay, preferred_element_type=jnp.float32)
    grad_query = weight_grad(normed_one, grad_query_rows)
    grad_key = weight_grad(normed_one, grad_key_rows)
    grad_value = weight_grad(normed_one, grad_value_rows)
    grad_outgate = weight_grad(normed_one, grad_gate_rows)
    back_one = (
        project_back(grad_query_rows, mat_query)
        + project_back(grad_key_rows, mat_key)
        + project_back(grad_value_rows, mat_value)
        + project_back(grad_gate_rows, mat_outgate)
    )
    back_full, rank_full, grad_headnorm_tp = (
        lax.psum(back_one.astype(jnp.bfloat16), "tp").astype(jnp.float32),
        lax.psum(rank_part.astype(jnp.bfloat16), "tp").astype(jnp.float32),
        lax.psum(headnorm_part.astype(jnp.bfloat16), "tp").astype(jnp.float32),
    )
    grad_rank = rank_full.astype(jnp.bfloat16)
    grad_lowrank = weight_grad(normed_one, grad_rank)
    norm_one_grad = back_full + project_back(grad_rank, mat_lowrank)
    grad_prenorm = jnp.sum(norm_one_grad * resid_in * scale_one, axis=(0, 1))
    grad_tokens = (grad_mid + norm_back(norm_one_grad, resid_in, scale_one, gain_first)).astype(
        jnp.bfloat16
    )
    owned = (
        lax.psum_scatter(
            grad_prenorm.astype(jnp.bfloat16), "fsdp", scatter_dimension=0, tiled=True
        ).astype(jnp.float32),
        lax.psum_scatter(
            grad_query.astype(jnp.bfloat16), "fsdp", scatter_dimension=0, tiled=True
        ).astype(jnp.float32),
        lax.psum_scatter(
            grad_key.astype(jnp.bfloat16), "fsdp", scatter_dimension=0, tiled=True
        ).astype(jnp.float32),
        lax.psum_scatter(
            grad_value.astype(jnp.bfloat16), "fsdp", scatter_dimension=0, tiled=True
        ).astype(jnp.float32),
        lax.psum_scatter(
            grad_outgate.astype(jnp.bfloat16), "fsdp", scatter_dimension=0, tiled=True
        ).astype(jnp.float32),
        lax.psum_scatter(
            grad_lowrank.astype(jnp.bfloat16), "fsdp", scatter_dimension=0, tiled=True
        ).astype(jnp.float32),
        lax.psum_scatter(
            grad_output.astype(jnp.bfloat16), "fsdp", scatter_dimension=1, tiled=True
        ).astype(jnp.float32),
        lax.psum_scatter(
            grad_postnorm.astype(jnp.bfloat16), "fsdp", scatter_dimension=0, tiled=True
        ).astype(jnp.float32),
        lax.psum_scatter(
            grad_gate.astype(jnp.bfloat16), "fsdp", scatter_dimension=0, tiled=True
        ).astype(jnp.float32),
        lax.psum_scatter(
            grad_up.astype(jnp.bfloat16), "fsdp", scatter_dimension=0, tiled=True
        ).astype(jnp.float32),
        lax.psum_scatter(
            grad_down.astype(jnp.bfloat16), "fsdp", scatter_dimension=1, tiled=True
        ).astype(jnp.float32),
    )
    owned = (
        lax.psum(owned[0].astype(jnp.bfloat16), "ctx").astype(jnp.float32),
        lax.psum(owned[1].astype(jnp.bfloat16), "ctx").astype(jnp.float32),
        lax.psum(owned[2].astype(jnp.bfloat16), "ctx").astype(jnp.float32),
        lax.psum(owned[3].astype(jnp.bfloat16), "ctx").astype(jnp.float32),
        lax.psum(owned[4].astype(jnp.bfloat16), "ctx").astype(jnp.float32),
        lax.psum(owned[5].astype(jnp.bfloat16), "ctx").astype(jnp.float32),
        lax.psum(owned[6].astype(jnp.bfloat16), "ctx").astype(jnp.float32),
        lax.psum(owned[7].astype(jnp.bfloat16), "ctx").astype(jnp.float32),
        lax.psum(owned[8].astype(jnp.bfloat16), "ctx").astype(jnp.float32),
        lax.psum(owned[9].astype(jnp.bfloat16), "ctx").astype(jnp.float32),
        lax.psum(owned[10].astype(jnp.bfloat16), "ctx").astype(jnp.float32),
    )
    decay_sum, bias_sum, headnorm_sum = lax.psum(
        (grad_decay, grad_bias, grad_headnorm_tp), ("fsdp", "ctx")
    )
    return (
        block_out,
        grad_tokens,
        owned[0],
        owned[1],
        owned[2],
        owned[3],
        owned[4],
        owned[5],
        decay_sum,
        bias_sum,
        headnorm_sum,
        owned[6],
        owned[7],
        owned[8],
        owned[9],
        owned[10],
    )


def solution(mesh):
    in_specs = (
        P("fsdp", "ctx", None),
        P("fsdp", "ctx"),
        P("fsdp"),
        P("fsdp", "tp"),
        P("fsdp", "tp"),
        P("fsdp", "tp"),
        P("fsdp", "tp"),
        P("fsdp", None),
        P(None, "tp"),
        P("tp"),
        P(),
        P("tp", "fsdp"),
        P("fsdp"),
        P("fsdp", "tp"),
        P("fsdp", "tp"),
        P("tp", "fsdp"),
        P("fsdp", "ctx", None),
    )
    out_specs = (
        P("fsdp", "ctx", None),
        P("fsdp", "ctx", None),
        P("fsdp"),
        P("fsdp", "tp"),
        P("fsdp", "tp"),
        P("fsdp", "tp"),
        P("fsdp", "tp"),
        P("fsdp", None),
        P(None, "tp"),
        P("tp"),
        P(),
        P("tp", "fsdp"),
        P("fsdp"),
        P("fsdp", "tp"),
        P("fsdp", "tp"),
        P("tp", "fsdp"),
    )
    return jax.shard_map(body, mesh=mesh, in_specs=in_specs, out_specs=out_specs, check_vma=False)
```

profile of v0, /device:TPU:0, one launch (start us, length us, event | category | flops | bytes accessed | tf_op | source)
XLA Modules:
  0.0 1287.3 jit_solution(14076927658923731034)
XLA Ops:
  9.2 5.4 collective-permute-start
  15.3 11.2 all-gather.4
  28.6 13.2 %all_gather.54 = bf16[1024,16]{0,1:T(8,128)(2,1)S(1)} all-gather(bf16[256,16]{0,1:T(8,128)(2,1)S(1)} %copy-done.52), channel_id=1, replica_groups=mesh['fsdp'=4,'ctx'=4,'tp'=2] {'fsdp'}, dimensions={0}, use_global_device_ids=true | all-gather | bytes 40960 | tf_op jit(solution)/shard_map/all_gather | solution.py:193
  47.9 19.2 %all_gather.56 = bf16[1024,256]{1,0:T(8,128)(2,1)S(1)} all-gather(bf16[256,256]{1,0:T(8,128)(2,1)S(1)} %copy-done.43), channel_id=1, replica_groups=mesh['fsdp'=4,'ctx'=4,'tp'=2] {'fsdp'}, dimensions={0}, use_global_device_ids=true | all-gather | bytes 655360 | tf_op jit(solution)/shard_map/all_gather | solution.py:190
  74.0 3.7 multiply_bitcast_fusion
  77.7 3.5 convolution_convert_fusion.5
  82.7 3.4 fusion.146
  90.5 14.7 %all_gather.60 = bf16[1024,256]{1,0:T(8,128)(2,1)S(1)} all-gather(bf16[256,256]{1,0:T(8,128)(2,1)S(1)} %copy-done.44), channel_id=1, replica_groups=mesh['fsdp'=4,'ctx'=4,'tp'=2] {'fsdp'}, dimensions={0}, use_global_device_ids=true | all-gather | bytes 655360 | tf_op jit(solution)/shard_map/all_gather | solution.py:189
  113.9 7.2 all-gather
  122.8 3.9 fusion.171
  129.9 149.2 %while.71 = (s32[]{:T(128)}, f32[1,2,128,256]{3,2,1,0:T(8,128)S(1)}, s32[1]{0:T(128)}, f32[16,1,2,64,256]{4,3,0,2,1:T(8,128)S(1)}, f32[16,1,2,128,256]{4,3,2,1,0...) while((s32[]{:T(128)}, ...), condition=%wide.region_7.8_spmd.clone, body=%wide.region_5.7_spmd.clone.sunk | while | flops 139776512 | bytes 2880203 | solution.py:101
  284.6 4.9 convolution_bitcast_fusion.3
  291.6 9.9 all-gather.5
  301.5 18.9 %all-reduce.18.cloned.1.call-done = f32[1,1024,1024]{2,1,0:T(8,128)} async-done(((f32[1,1024,1024]{2,1,0:T(8,128)}), f32[1,1024,1024]{2,1,0:T(8,128)}) %all-reduce.18.cloned.1.call-update) | async-done | bytes 4194320 | tf_op jit(solution)/shard_map/psum | solution.py:262
  320.4 3.5 multiply_reduce_fusion.1
  327.6 54.7 %all-gather.20.cloned.1.call-done = bf16[1024,1408]{1,0:T(8,128)(2,1)} async-done(((bf16[256,1408]{1,0:T(8,128)(2,1)}), bf16[1024,1408]{1,0:T(8,128)(2,1)}) %all-gather.20.cloned.1.call-update) | async-done | bytes 2883600 | tf_op jit(solution)/shard_map/all_gather | solution.py:196
  382.3 8.3 fusion.172
  390.7 51.2 %all-gather.22.cloned.1.call-done = bf16[1024,1408]{1,0:T(8,128)(2,1)} async-done(((bf16[256,1408]{1,0:T(8,128)(2,1)}), bf16[1024,1408]{1,0:T(8,128)(2,1)}) %all-gather.22.cloned.1.call-update) | async-done | bytes 2883600 | tf_op jit(solution)/shard_map/all_gather | solution.py:197
  441.9 8.4 fusion.173
  450.2 51.1 %all-gather.24.cloned.1.call-done = bf16[1408,1024]{1,0:T(8,128)(2,1)} async-done(((bf16[1408,256]{1,0:T(8,128)(2,1)}), bf16[1408,1024]{1,0:T(8,128)(2,1)}) %all-gather.24.cloned.1.call-update) | async-done | bytes 2883600 | tf_op jit(solution)/shard_map/all_gather | solution.py:198
  501.4 11.4 multiply_convert_fusion
  512.8 3.4 fusion.174
  516.7 4.7 fusion.117
  521.5 8.0 all-gather.3
  529.5 11.4 all-reduce.20.cloned.1.call-done
  541.0 4.3 fusion.111
  565.5 232.2 %while.72 = (s32[]{:T(128)}, f32[1,2,128,256]{2,3,1,0:T(8,128)S(1)}, f32[16,1,2,64,128]{4,3,0,2,1:T(8,128)}, f32[16,1,2,64,128]{4,3,0,2,1:T(8,128)}, f32[16,1,2,...) while((s32[]{:T(128)}, ...), condition=%wide.region_22.23_spmd.clone, body=%wide.region_15.22_spmd.clone.sunk | while | flops 292794880 | bytes 8436249 | solution.py:101
  797.8 10.6 all-gather.2
  811.6 8.7 fusion.166
  827.9 4.8 fusion.131
  835.7 3.9 fusion.119
  845.2 3.6 convolution_convert_fusion.3
  849.2 7.6 convolution_convert_fusion.2
  856.9 7.6 convolution_convert_fusion.1
  864.5 7.3 convolution_convert_fusion
  872.1 7.6 convert_bitcast_fusion.1
  900.1 3.5 all-reduce.11
  904.8 17.6 %reduce-scatter.14.cloned.1.call-done = bf16[256,512]{1,0:T(8,128)(2,1)} async-done(((bf16[1024,512]{1,0:T(8,128)(2,1)}), bf16[256,512]{1,0:T(8,128)(2,1)}) %reduce-scatter.14.cloned.1.call-update) | async-done | bytes 262160 | tf_op jit(solution)/shard_map/reduce_scatter | solution.py:345
  922.4 27.9 %reduce-scatter.16.cloned.1.call-done = bf16[256,512]{1,0:T(8,128)(2,1)} async-done(((bf16[1024,512]{1,0:T(8,128)(2,1)}), bf16[256,512]{1,0:T(8,128)(2,1)}) %reduce-scatter.16.cloned.1.call-update) | async-done | bytes 262160 | tf_op jit(solution)/shard_map/reduce_scatter | solution.py:348
  950.3 57.1 %reduce-scatter.22.cloned.1.call-done = bf16[256,1408]{1,0:T(8,128)(2,1)} async-done(((bf16[1024,1408]{1,0:T(8,128)(2,1)}), bf16[256,1408]{1,0:T(8,128)(2,1)}) %reduce-scatter.22.cloned.1.call-update) | async-done | bytes 720912 | tf_op jit(solution)/shard_map/reduce_scatter | solution.py:360
  1007.4 58.4 %reduce-scatter.24.cloned.1.call-done = bf16[256,1408]{1,0:T(8,128)(2,1)} async-done(((bf16[1024,1408]{1,0:T(8,128)(2,1)}), bf16[256,1408]{1,0:T(8,128)(2,1)}) %reduce-scatter.24.cloned.1.call-update) | async-done | bytes 720912 | tf_op jit(solution)/shard_map/reduce_scatter | solution.py:363
  1065.8 58.3 %reduce-scatter.26.cloned.1.call-done = bf16[1408,256]{1,0:T(8,128)(2,1)} async-done(((bf16[1408,1024]{1,0:T(8,128)(2,1)}), bf16[1408,256]{1,0:T(8,128)(2,1)}) %reduce-scatter.26.cloned.1.call-update) | async-done | bytes 720912 | tf_op jit(solution)/shard_map/reduce_scatter | solution.py:366
  1125.6 75.9 %all-reduce.7 = (f32[16,256]{1,0:T(8,128)}, f32[256]{0:T(256)}, f32[256]{0:T(256)}) all-reduce(f32[16,256]{1,0:T(8,128)S(1)} %fusion.177, f32[256]{0:T(256)S(1)} %get-tuple-element.889, bf16[256]{0:T(256)(128)(2,1)S(1)} %get-tuple-element.884), channel_id=1, replica_groups=mesh['fsdp'=4,'ctx'=4,'tp'=2] {'fsdp','ctx'}, use_global_device_ids=true, to_apply=%region_45.46 | all-reduce | flops 4608 | bytes 36352 | tf_op jit(solution)/shard_map/psum | solution.py:383
  1201.5 5.1 fusion.115
  1206.6 8.6 all-reduce.10
  1215.4 8.8 all-reduce.8
  1225.9 5.1 add_convert_fusion.2
  1234.5 36.9 %all-reduce.22.cloned.1.call-done = (bf16[256,256]{1,0:T(8,128)(2,1)}, bf16[256,256]{1,0:T(8,128)(2,1)}, bf16[256,512]{1,0:T(8,128)(2,1)}, bf16[256,512]{1,0:T(8...) async-done(((bf16[256,256]{1,0:T(8,128)(2,1)}, bf16[256,256]{1,0:T(8,128)(2,1)}, ...) | async-done | bytes 3211280 | tf_op jit(solution)/shard_map/psum | solution.py:372
  (1025 shorter events, 461.9 us)
Async XLA Ops:
  7.2 36.0 %copy-start = (bf16[16,256]{1,0:T(8,128)(2,1)S(1)}, bf16[16,256]{1,0:T(8,128)(2,1)}, u32[]{:S(2)}) copy-start(bf16[16,256]{1,0:T(8,128)(2,1)} %param.33) | copy-start | bytes 24580
  7.2 34.7 %copy-start.3 = (bf16[1,1024,1024]{2,1,0:T(8,128)(2,1)S(1)}, bf16[1,1024,1024]{2,1,0:T(8,128)(2,1)}, u32[]{:S(2)}) copy-start(bf16[1,1024,1024]{2,1,0:T(8,128)(2,1)} %param.25) | copy-start | bytes 6291460
  7.2 21.4 %copy-start.52 = (bf16[256,16]{0,1:T(8,128)(2,1)S(1)}, bf16[256,16]{0,1:T(8,128)(2,1)}, u32[]{:S(2)}) copy-start(bf16[256,16]{0,1:T(8,128)(2,1)} %param.32) | copy-start | bytes 24580
  7.2 34.7 %copy-start.57 = (bf16[256]{0:T(256)(128)(2,1)S(1)}, bf16[256]{0:T(256)(128)(2,1)}, u32[]{:S(2)}) copy-start(bf16[256]{0:T(256)(128)(2,1)} %param.34) | copy-start | bytes 1540
  7.2 70.5 %all-gather.14.cloned.1.call-start = ((), (), s32[]{:S(2)}) async-start(), calls=%async_computation.9 | async-start | bytes 1310720 | tf_op jit(solution)/shard_map/all_gather | solution.py:191
  8.0 114.8 %all-gather.16.cloned.1.call-start = ((), (), s32[]{:S(2)}) async-start(), calls=%async_computation.10 | async-start | bytes 1310720 | tf_op jit(solution)/shard_map/all_gather | solution.py:192
  9.2 63.5 %collective-permute-start = (s32[1]{0:T(128)}, s32[1]{0:T(128)}, u32[]{:S(2)}, u32[]{:S(2)}) collective-permute-start(s32[1]{0:T(128)} %bitcast.14), channel_id=1, source_target_pairs={{0,2},{2,4},{4,6},{1,3},{3,5},{5,7},{8,10},{10,12},{12,14},{9,11},... | collective-permute-start | bytes 20 | tf_op jit(solution)/shard_map/ppermute | solution.py:19
  14.6 115.0 %all-gather.26.cloned.1.call-start = ((), (), s32[]{:S(2)}) async-start(), calls=%async_computation.26 | async-start | bytes 1310720 | tf_op jit(solution)/shard_map/all_gather | solution.py:24
  26.5 15.9 %copy-start.47 = (f32[4,1,256]{2,1,0:T(1,128)}, f32[4,1,256]{2,1,0:T(1,128)S(1)}, u32[]{:S(2)}) copy-start(f32[4,1,256]{2,1,0:T(1,128)S(1)} %convert_element_type.448) | copy-start | bytes 12292
  28.6 13.8 %copy-start.49 = (f32[1024]{0:T(1024)}, f32[1024]{0:T(1024)S(1)}, u32[]{:S(2)}) copy-start(f32[1024]{0:T(1024)S(1)} %add_rsqrt_fusion.2) | copy-start | bytes 12292
  45.3 21.7 %copy-start.6 = (bf16[1024,1024]{1,0:T(8,128)(2,1)S(1)}, bf16[1024,1024]{1,0:T(8,128)(2,1)}, u32[]{:S(2)}) copy-start(bf16[1024,1024]{1,0:T(8,128)(2,1)} %copy-done.5) | copy-start | bytes 6291460
  70.0 7.7 copy-start.15
  82.7 38.3 %copy-start.13 = (bf16[1,1024,2,256]{3,1,2,0:T(8,128)(2,1)}, bf16[1,1024,2,256]{3,1,2,0:T(8,128)(2,1)S(1)}, u32[]{:S(2)}) copy-start(bf16[1,1024,2,256]{3,1,2,0:T(8,128)(2,1)S(1)} %copy.216) | copy-start | bytes 3145732
  86.2 198.4 %all-gather.18.cloned.1.call-start = ((), (), s32[]{:S(2)}) async-start(), calls=%async_computation.11 | async-start | bytes 1310720 | tf_op jit(solution)/shard_map/all_gather | solution.py:194
  86.8 233.7 %all-reduce.18.cloned.1.call-start = ((), (), s32[]{:S(2)}) async-start(), calls=%async_computation.12 | async-start | bytes 8388608 | tf_op jit(solution)/shard_map/psum | solution.py:262
  107.7 6.1 copy-start.58
  289.5 92.8 %all-gather.20.cloned.1.call-start = ((), (), s32[]{:S(2)}) async-start(), calls=%async_computation.13 | async-start | bytes 3604480 | tf_op jit(solution)/shard_map/all_gather | solution.py:196
  290.0 151.8 %all-gather.22.cloned.1.call-start = ((), (), s32[]{:S(2)}) async-start(), calls=%async_computation.14 | async-start | bytes 3604480 | tf_op jit(solution)/shard_map/all_gather | solution.py:197
  290.8 210.6 %all-gather.24.cloned.1.call-start = ((), (), s32[]{:S(2)}) async-start(), calls=%async_computation.15 | async-start | bytes 3604480 | tf_op jit(solution)/shard_map/all_gather | solution.py:198
  291.5 249.4 %all-reduce.20.cloned.1.call-start = ((), (), s32[]{:S(2)}) async-start(), calls=%async_computation.16 | async-start | bytes 4194304 | tf_op jit(solution)/shard_map/psum | solution.py:282
  501.4 11.4 copy-start.53
  512.8 3.9 copy-start.54
  521.4 383.3 %reduce-scatter.12.cloned.1.call-start = ((), (), s32[]{:S(2)}) async-start(), calls=%async_computation.18 | async-start | bytes 655360 | tf_op jit(solution)/shard_map/reduce_scatter | solution.py:342
  541.0 4.3 copy-start.2
  541.0 4.7 copy-start.19
  797.8 11.4 copy-start.14
  811.6 9.5 copy-start.7
  822.8 82.0 %reduce-scatter.10.cloned.1.call-start = ((), (), s32[]{:S(2)}) async-start(), calls=%async_computation.17 | async-start | bytes 655360 | tf_op jit(solution)/shard_map/reduce_scatter | solution.py:339
  827.9 76.9 %reduce-scatter.20.cloned.1.call-start = ((), (), s32[]{:S(2)}) async-start(), calls=%async_computation.22 | async-start | bytes 1310720 | tf_op jit(solution)/shard_map/reduce_scatter | solution.py:354
  832.8 89.6 %reduce-scatter.14.cloned.1.call-start = ((), (), s32[]{:S(2)}) async-start(), calls=%async_computation.19 | async-start | bytes 1310720 | tf_op jit(solution)/shard_map/reduce_scatter | solution.py:345
  842.8 107.4 %reduce-scatter.16.cloned.1.call-start = ((), (), s32[]{:S(2)}) async-start(), calls=%async_computation.20 | async-start | bytes 1310720 | tf_op jit(solution)/shard_map/reduce_scatter | solution.py:348
  848.7 158.7 %reduce-scatter.22.cloned.1.call-start = ((), (), s32[]{:S(2)}) async-start(), calls=%async_computation.23 | async-start | bytes 3604480 | tf_op jit(solution)/shard_map/reduce_scatter | solution.py:360
  856.8 208.9 %reduce-scatter.24.cloned.1.call-start = ((), (), s32[]{:S(2)}) async-start(), calls=%async_computation.24 | async-start | bytes 3604480 | tf_op jit(solution)/shard_map/reduce_scatter | solution.py:363
  864.5 259.6 %reduce-scatter.26.cloned.1.call-start = ((), (), s32[]{:S(2)}) async-start(), calls=%async_computation.25 | async-start | bytes 3604480 | tf_op jit(solution)/shard_map/reduce_scatter | solution.py:366
  871.9 7.9 copy-start.26
  871.9 329.6 %all-reduce.24.cloned.1.call-start = ((), (), s32[]{:S(2)}) async-start(), calls=%async_computation.28 | async-start | bytes 8388608 | tf_op jit(solution)/shard_map/psum | solution.py:271
  872.1 7.6 copy-start.28
  886.8 328.6 %reduce-scatter.18.cloned.1.call-start = ((), (), s32[]{:S(2)}) async-start(), calls=%async_computation.21 | async-start | bytes 40960 | tf_op jit(solution)/shard_map/reduce_scatter | solution.py:351
  904.6 219.5 %copy-start.60 = (u32[32]{0:T(128)S(1)}, u32[32]{0:T(128)}, u32[]{:S(2)}) copy-start(u32[32]{0:T(128)} %constant.205) | copy-start | bytes 388
  904.6 220.8 %copy-start.40 = (bf16[1024,16]{0,1:T(8,128)(2,1)S(1)}, bf16[1024,16]{0,1:T(8,128)(2,1)}, u32[]{:S(2)}) copy-start(bf16[1024,16]{0,1:T(8,128)(2,1)} %copy-done.39) | copy-start | bytes 98308
  904.6 296.9 %copy-start.4 = (bf16[1,1024,1024]{2,1,0:T(8,128)(2,1)S(1)}, bf16[1,1024,1024]{2,1,0:T(8,128)(2,1)}, u32[]{:S(2)}) copy-start(bf16[1,1024,1024]{2,1,0:T(8,128)(2,1)} %param.25) | copy-start | bytes 6291460
  904.6 296.9 %copy-start.42 = (bf16[1024,16]{0,1:T(8,128)(2,1)S(1)}, bf16[1024,16]{0,1:T(8,128)(2,1)}, u32[]{:S(2)}) copy-start(bf16[1024,16]{0,1:T(8,128)(2,1)} %copy-done.41) | copy-start | bytes 98308
  904.6 296.9 %copy-start.48 = (f32[4,1,256]{2,1,0:T(1,128)S(1)}, f32[4,1,256]{2,1,0:T(1,128)}, u32[]{:S(2)}) copy-start(f32[4,1,256]{2,1,0:T(1,128)} %copy-done.47) | copy-start | bytes 12292
  904.6 296.9 %copy-start.50 = (f32[1024]{0:T(1024)S(1)}, f32[1024]{0:T(1024)}, u32[]{:S(2)}) copy-start(f32[1024]{0:T(1024)} %copy-done.49) | copy-start | bytes 12292
  904.6 366.8 %all-reduce.22.cloned.1.call-start = ((), (), s32[]{:S(2)}) async-start(), calls=%async_computation.27 | async-start | bytes 6422528 | tf_op jit(solution)/shard_map/psum | solution.py:372
  1225.9 5.1 copy-start.12
  1225.9 6.1 copy-start.22
  1275.1 4.5 copy-start.45
  (36 other events, 79.7 us)
Sparse Core Ops, SparseCore 0:
  9.6 31.1 all-gather.13
  42.4 32.1 all-gather.15
  86.3 24.6 all-gather.25
  112.4 30.1 all-gather.17
  289.6 30.8 all-reduce.17
  321.9 60.3 all-gather.19
  384.0 57.8 all-gather.21
  443.5 57.8 all-gather.23
  521.5 19.3 all-reduce.19
  822.9 21.4 reduce-scatter.11
  846.7 19.9 reduce-scatter.9
  868.8 25.3 reduce-scatter.19
  896.5 25.7 reduce-scatter.13
  924.5 25.7 reduce-scatter.15
  952.5 54.8 reduce-scatter.21
  1009.7 56.0 reduce-scatter.23
  1068.0 56.0 reduce-scatter.25
  1127.2 28.3 all-reduce.23
  1158.5 20.0 reduce-scatter.17
  1182.8 88.5 all-reduce.21
where the time goes:
time: 1310 us; the launch traced here: 1290 us
  waiting for transfers between devices  447 us (34%)
  matrix products  268 us (20%)
  local copies, waits for them, and re-layouts  193 us (15%)
  blocking collectives  191 us (15%)
  other arithmetic  120 us (9%)
  loops' own time  44.3 us (3%)
  between operations  17.3 us (1%)
    psum x1, blocking collectives, body(): lax.psum((grad_decay, grad_bias, grad_headnorm_tp), ('fsdp', 'ctx'))  75.9 us
    squeeze x112, local copies, waits for them, and re-layouts, run_blocks(): lax.scan(jax.checkpoint(block_step), (running, prev_ids), (split_rows(que...  71 us
    reduce_scatter x1, waiting for transfers between devices, body(): lax.psum_scatter(grad_up.astype(jnp.bfloat16), 'fsdp', scatter_dimension=...  58.4 us
    reduce_scatter x1, waiting for transfers between devices, body(): lax.psum_scatter(grad_down.astype(jnp.bfloat16), 'fsdp', scatter_dimensio...  58.3 us
    reduce_scatter x1, waiting for transfers between devices, body(): lax.psum_scatter(grad_gate.astype(jnp.bfloat16), 'fsdp', scatter_dimensio...  57.1 us
    all_gather x1, waiting for transfers between devices, body(): lax.all_gather(w_gate, 'fsdp', axis=0, tiled=True)  54.7 us
    all_gather x1, waiting for transfers between devices, body(): lax.all_gather(w_up, 'fsdp', axis=0, tiled=True)  51.2 us
    all_gather x1, waiting for transfers between devices, body(): lax.all_gather(w_down, 'fsdp', axis=1, tiled=True)  51.1 us
  transfers between devices with their start and end apart: 21, of which 11 were waited for; matrix products, arithmetic and copies ran while one was open for 23% of the time, Pallas kernels for 0%

commit v1 on v0

v1 whole, which is shorter than its diff:
```python
import functools

import jax
import jax.numpy as jnp
from jax import lax
from jax.experimental import pallas as pl
from jax.experimental.pallas import tpu as pltpu
from jax.sharding import PartitionSpec as P

KH = 128
VH = 256
BLOCK = 64


EPSILON = 1e-06
HEAD_FLOOR = 1.0
NORMALIZER = 16.0
SCALE = KH ** (-0.5)
BF = jnp.bfloat16
F32 = jnp.float32
VMEM_LIMIT = 50 * 1024 * 1024


def mm(left, right, left_dim=1, right_dim=0):
    return lax.dot_general(
        left, right, (((left_dim,), (right_dim,)), ((), ())), preferred_element_type=F32
    )


def split_hi_lo(array):
    hi = array.astype(BF)
    return hi, (array - hi.astype(F32)).astype(BF)


def tri(rows, inclusive_lower, copies):
    at_row = lax.broadcasted_iota(jnp.int32, (rows, rows), 0)
    at_col = lax.broadcasted_iota(jnp.int32, (rows, rows), 1)
    mask = at_row >= at_col if inclusive_lower else at_row <= at_col
    square = mask.astype(F32).astype(BF)
    return jnp.concatenate([square] * copies, axis=1)


def block_ids(ids_smem, prev_smem, block):
    last = ids_smem[block * BLOCK + BLOCK - 1]
    before = ids_smem[jnp.maximum(block * BLOCK - 1, 0)]
    prev = jnp.where(block == 0, prev_smem[0], before)
    return last, prev


def ending_kernel(heads, ids_s, prev_s, ids_c, key, value, decay, total_out, state_out, sum_out):
    count = key.shape[0] // BLOCK
    state_out[...] = jnp.zeros_like(state_out)
    sum_out[...] = jnp.zeros_like(sum_out)
    lower = tri(BLOCK, True, 3)

    def step(block, _):
        rows = pl.ds(pl.multiple_of(block * BLOCK, BLOCK), BLOCK)
        last, prev = block_ids(ids_s, prev_s, block)
        keep = (ids_c[rows, :] == last).astype(F32)
        survive = (last == prev).astype(F32)
        decay_rows = decay[rows, :]
        hi, rest = decay_rows.astype(BF), decay_rows
        rest = rest - hi.astype(F32)
        mid, low = split_hi_lo(rest)
        total = mm(lower, jnp.concatenate([hi, mid, low], axis=0))
        total_out[rows, :] = total
        final = total[BLOCK - 1 : BLOCK, :]
        sum_out[...] += final
        tail = (key[rows, :].astype(F32) * jnp.exp(final - total) * keep).astype(BF)
        through = survive * jnp.exp(final)
        for head in range(heads):
            kc = slice(head * KH, (head + 1) * KH)
            vc = slice(head * VH, (head + 1) * VH)
            fresh = mm(value[rows, vc], tail[:, kc], 0, 0)
            state_out[vc, :] = state_out[vc, :] * through[:, kc] + fresh
        return 0

    lax.fori_loop(0, count, step, 0, unroll=4)


def forward_kernel(
    heads,
    ids_s,
    prev_s,
    ids_c,
    ids_r,
    query,
    key,
    value,
    total_in,
    gate,
    gain,
    state_in,
    mixed_out,
    gated_out,
    states_out,
    state,
):
    count = key.shape[0] // BLOCK
    state[...] = state_in[...]
    later = lax.broadcasted_iota(jnp.int32, (BLOCK, BLOCK), 0)
    earlier = lax.broadcasted_iota(jnp.int32, (BLOCK, BLOCK), 1)

    def step(block, _):
        rows = pl.ds(pl.multiple_of(block * BLOCK, BLOCK), BLOCK)
        last, prev = block_ids(ids_s, prev_s, block)
        ids = ids_c[rows, :]
        linked = (ids == ids_r[pl.ds(block, 1), :]) & (later >= earlier)
        keep = (ids == last).astype(F32)
        alive = (ids == prev).astype(F32) * SCALE
        survive = (last == prev).astype(F32)
        total = total_in[rows, :]
        final = total[BLOCK - 1 : BLOCK, :]
        anchor = total[BLOCK // 2 : BLOCK // 2 + 1, :]
        query_f = query[rows, :].astype(F32)
        key_f = key[rows, :].astype(F32)
        query_scaled = (query_f * SCALE * jnp.exp(total - anchor)).astype(BF)
        key_scaled = (key_f * jnp.exp(anchor - total)).astype(BF)
        reach = (query_f * jnp.exp(total) * alive).astype(BF)
        tail = (key_f * jnp.exp(final - total) * keep).astype(BF)
        through = survive * jnp.exp(final)
        for head in range(heads):
            kc = slice(head * KH, (head + 1) * KH)
            vc = slice(head * VH, (head + 1) * VH)
            value_rows = value[rows, vc]
            scores = mm(query_scaled[:, kc], key_scaled[:, kc], 1, 1)
            scores = jnp.where(linked, scores, 0.0).astype(BF)
            now = state[vc, :]
            now_b = now.astype(BF)
            states_out[block, vc, :] = now_b
            out = mm(scores, value_rows) + mm(reach[:, kc], now_b, 1, 1)
            mixed_out[rows, vc] = out
            state[vc, :] = now * through[:, kc] + mm(value_rows, tail[:, kc], 0, 0)
            unit = out * lax.rsqrt(jnp.mean(out * out, axis=-1, keepdims=True) + HEAD_FLOOR)
            gate_rows = gate[rows, vc]
            swish = gate_rows * jax.nn.sigmoid(gate_rows)
            gated_out[rows, vc] = (unit * gain[...] * swish).astype(BF)
        return 0

    lax.fori_loop(0, count, step, 0, unroll=4)


def back_start_kernel(
    heads,
    ids_s,
    prev_s,
    ids_c,
    query,
    total_in,
    gate,
    gain,
    mixed,
    grad_gated,
    grad_mixed_out,
    grad_gate_out,
    headnorm_out,
    adjoint_out,
):
    count = query.shape[0] // BLOCK
    adjoint_out[...] = jnp.zeros_like(adjoint_out)
    headnorm_out[...] = jnp.zeros_like(headnorm_out)

    def step(turn, _):
        block = count - 1 - turn
        rows = pl.ds(pl.multiple_of(block * BLOCK, BLOCK), BLOCK)
        last, prev = block_ids(ids_s, prev_s, block)
        alive = (ids_c[rows, :] == prev).astype(F32) * SCALE
        survive = (last == prev).astype(F32)
        total = total_in[rows, :]
        final = total[BLOCK - 1 : BLOCK, :]
        reach = (query[rows, :].astype(F32) * jnp.exp(total) * alive).astype(BF)
        through = survive * jnp.exp(final)
        gain_row = gain[...]
        for head in range(heads):
            kc = slice(head * KH, (head + 1) * KH)
            vc = slice(head * VH, (head + 1) * VH)
            out = mixed[rows, vc]
            scale = lax.rsqrt(jnp.mean(out * out, axis=-1, keepdims=True) + HEAD_FLOOR)
            unit = out * scale
            gate_rows = gate[rows, vc]
            sig = jax.nn.sigmoid(gate_rows)
            swish = gate_rows * sig
            grad = grad_gated[rows, vc]
            grad_n = grad * unit
            headnorm_out[...] += jnp.sum(grad_n * swish, axis=0, keepdims=True)
            grad_gate_out[rows, vc] = (
                grad_n * gain_row * sig * (1.0 + gate_rows * (1.0 - sig))
            ).astype(BF)
            grad_unit = grad * gain_row * swish
            grad_mixed = scale * (
                grad_unit - unit * jnp.mean(grad_unit * unit, axis=-1, keepdims=True)
            )
            grad_mixed = grad_mixed.astype(BF)
            grad_mixed_out[rows, vc] = grad_mixed
            adjoint_out[vc, :] = adjoint_out[vc, :] * through[:, kc] + mm(
                grad_mixed, reach[:, kc], 0, 0
            )
        return 0

    lax.fori_loop(0, count, step, 0, unroll=4)


def backward_kernel(
    heads,
    ids_s,
    prev_s,
    ids_c,
    ids_r,
    query,
    key,
    value,
    total_in,
    grad_mixed,
    states,
    adjoint_in,
    grad_query_out,
    grad_key_out,
    grad_value_out,
    grad_decay_out,
    adjoint,
):
    count = key.shape[0] // BLOCK
    adjoint[...] = adjoint_in[...]
    later = lax.broadcasted_iota(jnp.int32, (BLOCK, BLOCK), 0)
    earlier = lax.broadcasted_iota(jnp.int32, (BLOCK, BLOCK), 1)
    upper = tri(BLOCK, False, 2)

    def step(turn, _):
        block = count - 1 - turn
        rows = pl.ds(pl.multiple_of(block * BLOCK, BLOCK), BLOCK)
        last, prev = block_ids(ids_s, prev_s, block)
        ids = ids_c[rows, :]
        linked = (ids == ids_r[pl.ds(block, 1), :]) & (later >= earlier)
        keep = (ids == last).astype(F32)
        alive = (ids == prev).astype(F32) * SCALE
        survive = (last == prev).astype(F32)
        total_all = total_in[rows, :]
        final_all = total_all[BLOCK - 1 : BLOCK, :]
        anchor_all = total_all[BLOCK // 2 : BLOCK // 2 + 1, :]
        for head in range(heads):
            kc = slice(head * KH, (head + 1) * KH)
            vc = slice(head * VH, (head + 1) * VH)
            total = total_all[:, kc]
            final = final_all[:, kc]
            anchor = anchor_all[:, kc]
            query_f = query[rows, kc].astype(F32)
            key_f = key[rows, kc].astype(F32)
            query_grow = SCALE * jnp.exp(total - anchor)
            key_grow = jnp.exp(anchor - total)
            reach_grow = jnp.exp(total) * alive
            tail_grow = jnp.exp(final - total) * keep
            through = survive * jnp.exp(final)
            query_scaled = (query_f * query_grow).astype(BF)
            key_scaled = (key_f * key_grow).astype(BF)
            reach = (query_f * reach_grow).astype(BF)
            tail = (key_f * tail_grow).astype(BF)
            value_rows = value[rows, vc]
            grad = grad_mixed[rows, vc]
            before = states[block, vc, :]
            after = adjoint[vc, :]
            after_b = after.astype(BF)
            scores = mm(query_scaled, key_scaled, 1, 1)
            scores = jnp.where(linked, scores, 0.0).astype(BF)
            grad_scores = mm(grad, value_rows, 1, 1)
            grad_scores = jnp.where(linked, grad_scores, 0.0).astype(BF)
            grad_query_scaled = mm(grad_scores, key_scaled)
            grad_key_scaled = mm(grad_scores, query_scaled, 0, 0)
            grad_reach = mm(grad, before)
            grad_tail = mm(value_rows, after_b)
            grad_query_out[rows, kc] = (
                grad_query_scaled * query_grow + grad_reach * reach_grow
            ).astype(BF)
            grad_key_out[rows, kc] = (grad_key_scaled * key_grow + grad_tail * tail_grow).astype(BF)
            grad_value_out[rows, vc] = (mm(scores, grad, 0, 0) + mm(tail, after_b, 1, 1)).astype(BF)
            tail_part = tail.astype(F32) * grad_tail
            grad_total = (
                query_scaled.astype(F32) * grad_query_scaled
                - key_scaled.astype(F32) * grad_key_scaled
                + reach.astype(F32) * grad_reach
                - tail_part
            )
            grad_final = jnp.sum(tail_part, axis=0, keepdims=True) + through * jnp.sum(
                before.astype(F32) * after, axis=0, keepdims=True
            )
            hi, low = split_hi_lo(grad_total)
            grad_decay_out[rows, kc] = (
                mm(upper, jnp.concatenate([hi, low], axis=0)) + grad_final
            )
            adjoint[vc, :] = after * through + mm(grad, reach, 0, 0)
        return 0

    lax.fori_loop(0, count, step, 0, unroll=2)


def call(kernel, outs, kinds, args, flops, scratch=()):
    spaces = {"s": pltpu.SMEM, "v": pltpu.VMEM}
    shapes = [jax.ShapeDtypeStruct(shape, kind) for shape, kind in outs]
    moved = sum(a.size * a.dtype.itemsize for a in list(args) + shapes)
    return pl.pallas_call(
        kernel,
        out_shape=shapes,
        in_specs=[pl.BlockSpec(memory_space=spaces[kind]) for kind in kinds],
        out_specs=[pl.BlockSpec(memory_space=pltpu.VMEM)] * len(outs),
        scratch_shapes=list(scratch),
        cost_estimate=pl.CostEstimate(flops=flops, bytes_accessed=moved, transcendentals=0),
        compiler_params=pltpu.CompilerParams(vmem_limit_bytes=VMEM_LIMIT),
    )(*args)


def ending_call(ids, prev, ids_col, key, value, decay):
    length, keys = key.shape
    heads = keys // KH
    return call(
        functools.partial(ending_kernel, heads),
        [((length, keys), F32), ((heads * VH, KH), F32), ((1, keys), F32)],
        "ssvvvv",
        (ids, prev, ids_col, key, value, decay),
        8 * 10**9,
    )


def forward_call(ids, prev, ids_col, ids_row, query, key, value, total, gate, gain, state):
    length, keys = key.shape
    heads = keys // KH
    return call(
        functools.partial(forward_kernel, heads),
        [
            ((length, heads * VH), F32),
            ((length, heads * VH), BF),
            ((length // BLOCK, heads * VH, KH), BF),
        ],
        "ssvvvvvvvvv",
        (ids, prev, ids_col, ids_row, query, key, value, total, gate, gain, state),
        20 * 10**9,
        [pltpu.VMEM((heads * VH, KH), F32)],
    )


def back_start_call(ids, prev, ids_col, query, total, gate, gain, mixed, grad_gated):
    length, keys = query.shape
    heads = keys // KH
    return call(
        functools.partial(back_start_kernel, heads),
        [
            ((length, heads * VH), BF),
            ((length, heads * VH), BF),
            ((1, VH), F32),
            ((heads * VH, KH), F32),
        ],
        "ssvvvvvvv",
        (ids, prev, ids_col, query, total, gate, gain, mixed, grad_gated),
        15 * 10**9,
    )


def backward_call(ids, prev, ids_col, ids_row, query, key, value, total, grad, states, adjoint):
    length, keys = key.shape
    heads = keys // KH
    return call(
        functools.partial(backward_kernel, heads),
        [
            ((length, keys), BF),
            ((length, keys), BF),
            ((length, heads * VH), BF),
            ((length, keys), F32),
        ],
        "ssvvvvvvvvv",
        (ids, prev, ids_col, ids_row, query, key, value, total, grad, states, adjoint),
        40 * 10**9,
        [pltpu.VMEM((heads * VH, KH), F32)],
    )


def swap(array, axis, bit):
    count = lax.axis_size(axis)
    return lax.ppermute(array, axis, [(i, i ^ bit) for i in range(count)])


def both(part):
    sent = part.astype(BF)
    return sent.astype(F32) + swap(sent, "tp", 1).astype(F32)


def pick(array, index, axis):
    return lax.dynamic_index_in_dim(array, index, axis, False)


def paired(mine, other, bit, axis):
    low = jnp.where(bit == 0, mine, other)
    high = jnp.where(bit == 0, other, mine)
    return jnp.stack([low, high], axis=axis)


def along_ctx(array):
    place = lax.axis_index("ctx")
    x_bit, y_bit = place % 2, place // 2
    half = array.shape[0] // 2

    def x_first(part):
        row = paired(part, swap(part, "ctx", 1), x_bit, -3)
        whole = paired(row, swap(row, "ctx", 2), y_bit, -4)
        return whole.reshape(*part.shape[:-2], 4, *part.shape[-2:])

    def y_first(part):
        row = paired(part, swap(part, "ctx", 2), y_bit, -3)
        whole = paired(row, swap(row, "ctx", 1), x_bit, -3)
        return whole.reshape(*part.shape[:-2], 4, *part.shape[-2:])

    return jnp.concatenate([x_first(array[:half]), y_first(array[half:])], axis=0)


def gather_rows(shard):
    rows, columns = shard.shape
    count, ctx = lax.axis_size("fsdp"), lax.axis_size("ctx")
    if ctx != 4 or count % 2:
        return lax.all_gather(shard, "fsdp", axis=0, tiled=True)
    part = lax.dynamic_slice_in_dim(shard, lax.axis_index("ctx") * (rows // ctx), rows // ctx, 0)
    if count > 4:
        pieces = lax.all_gather(part, "fsdp", axis=0)
    else:
        place = lax.axis_index("fsdp")
        pieces = jnp.zeros((count, *part.shape), part.dtype)
        pieces = lax.dynamic_update_index_in_dim(pieces, part, place, 0)
        for shift in range(1, count):
            moved = lax.ppermute(part, "fsdp", [(i, (i + shift) % count) for i in range(count)])
            pieces = lax.dynamic_update_index_in_dim(pieces, moved, (place - shift) % count, 0)
    return along_ctx(pieces).reshape(count * rows, columns)


def reduce_rows(grad):
    rows, columns = grad.shape
    count, ctx = lax.axis_size("fsdp"), lax.axis_size("ctx")
    grad = grad.astype(BF)
    if ctx != 4 or count % 2:
        own = lax.psum_scatter(grad, "fsdp", scatter_dimension=0, tiled=True)
        return lax.psum(own, "ctx").astype(F32)
    place = lax.axis_index("ctx")
    x_bit, y_bit = place % 2, place // 2
    size = rows // (count * ctx)
    blocks = grad.reshape(count, 2, 2, size, columns)
    half = count // 2

    def fold(array, bit, step, axis):
        theirs = swap(pick(array, 1 - bit, axis), "ctx", step)
        return (pick(array, bit, axis).astype(F32) + theirs.astype(F32)).astype(BF)

    first = fold(fold(blocks[:half], x_bit, 1, 2), y_bit, 2, 1)
    second = fold(fold(blocks[half:], y_bit, 2, 1), x_bit, 1, 1)
    partial = jnp.concatenate([first, second], axis=0)
    if count > 4:
        own = lax.psum_scatter(partial, "fsdp", scatter_dimension=0, tiled=False)
    else:
        at = lax.axis_index("fsdp")
        total = pick(partial, at, 0).astype(F32)
        for shift in range(1, count):
            sent = pick(partial, (at + shift) % count, 0)
            moved = lax.ppermute(sent, "fsdp", [(i, (i + shift) % count) for i in range(count)])
            total = total + moved.astype(F32)
        own = total.astype(BF)
    halves = own.reshape(2, size // 2, columns)
    whole = along_ctx(halves)
    return jnp.moveaxis(whole, 0, 1).reshape(ctx * size, columns).astype(F32)


def shifted(value, axis, steps):
    count = lax.axis_size(axis)
    initial, last = (max(0, -steps), min(count, count - steps))
    return lax.ppermute(value, axis, [(source, source + steps) for source in range(initial, last)])


def dot(left, right, left_dim=1, right_dim=0):
    return lax.dot_general(
        left, right, (((left_dim,), (right_dim,)), ((), ())), preferred_element_type=F32
    )


def rms_scale(rows):
    return lax.rsqrt(jnp.mean(rows * rows, axis=-1, keepdims=True) + EPSILON)


def norm_back(grad_normed, rows, scale, gain):
    inner_term = gain * grad_normed
    return scale * (
        inner_term - rows * scale * scale * jnp.mean(inner_term * rows, axis=-1, keepdims=True)
    )


def chain(decay, state, order, used):
    out = jnp.zeros_like(state[0])
    for source in order:
        out = jnp.where(used(source), decay[source] * out + state[source].astype(F32), out)
    return out


def body(
    tokens,
    doc_ids,
    prenorm,
    w_query,
    w_key,
    w_value,
    w_outgate,
    w_lowrank,
    w_decay,
    decay_bias,
    headnorm,
    w_output,
    postnorm,
    w_gate,
    w_up,
    w_down,
    cotangent,
):
    keys, values = w_query.shape[1], w_value.shape[1]
    rank, hidden_size = w_lowrank.shape[1], w_gate.shape[1]
    heads = keys // KH
    mixer_size = 2 * keys + 2 * values
    extra = -(rank + 2) % 128
    pad = jnp.zeros((prenorm.shape[0], extra), BF)
    mixer_pack = jnp.concatenate(
        [w_query, w_key, w_value, w_outgate, w_lowrank, prenorm[:, None], postnorm[:, None], pad],
        axis=1,
    )
    mixer_all = gather_rows(mixer_pack)
    mat_output = gather_rows(w_output.T).T
    mat_ffn = gather_rows(jnp.concatenate([w_gate, w_up], axis=1))
    mat_down_t = gather_rows(w_down.T)
    mat_lowrank = mixer_all[:, mixer_size : mixer_size + rank]
    gain_first = mixer_all[:, mixer_size + rank].astype(F32)
    gain_second = mixer_all[:, mixer_size + rank + 1].astype(F32)
    gain_head = headnorm.astype(F32)[None, :]

    place, pieces = lax.axis_index("ctx"), lax.axis_size("ctx")
    ids = doc_ids[0]
    last_id = ids[-1:]
    prev_id = shifted(last_id, "ctx", 1)
    link = (last_id == prev_id).astype(F32)
    ids_col, ids_row = ids[:, None], ids.reshape(-1, BLOCK)

    resid_in = tokens[0].astype(F32)
    scale_one = rms_scale(resid_in)
    normed_one = (resid_in * scale_one * gain_first).astype(BF)
    projected = dot(normed_one, mixer_all)
    query = projected[:, :keys].astype(BF)
    key = projected[:, keys : 2 * keys].astype(BF)
    value = projected[:, 2 * keys : 2 * keys + values].astype(BF)
    gate_pre = projected[:, 2 * keys + values : mixer_size]
    rank_act = projected[:, mixer_size : mixer_size + rank].astype(BF)
    decay_logit = dot(rank_act, w_decay) + decay_bias.astype(F32)
    log_decay = jax.nn.log_sigmoid(decay_logit) / NORMALIZER

    total, ending, decay_sum = ending_call(ids, prev_id, ids_col, key, value, log_decay)
    through = jnp.exp(decay_sum) * link
    through_all = lax.all_gather(through, "ctx")
    ending_all = lax.all_gather(ending, "ctx")
    columns = jnp.repeat(through_all.reshape(pieces, heads, 1, KH), VH, axis=2)
    columns = columns.reshape(pieces, heads * VH, KH)
    incoming = chain(columns, ending_all, range(pieces), lambda source: source < place)
    mixed, gated, states = forward_call(
        ids, prev_id, ids_col, ids_row, query, key, value, total, gate_pre, gain_head, incoming
    )

    resid_mid = resid_in + both(dot(gated, mat_output))
    scale_two = rms_scale(resid_mid)
    normed_two = (resid_mid * scale_two * gain_second).astype(BF)
    acts = dot(normed_two, mat_ffn)
    gate_act, up_act = acts[:, :hidden_size], acts[:, hidden_size:]
    ffn_sig = jax.nn.sigmoid(gate_act)
    silu_act = gate_act * ffn_sig
    hidden = (silu_act * up_act).astype(BF)
    block_out = (resid_mid + both(dot(hidden, mat_down_t, 1, 1))).astype(BF)
    cot = cotangent[0]
    grad_hidden = dot(cot, mat_down_t)
    grad_gate_act = (grad_hidden * up_act * ffn_sig * (1.0 + gate_act * (1.0 - ffn_sig))).astype(BF)
    grad_up_act = (grad_hidden * silu_act).astype(BF)
    grad_acts = jnp.concatenate([grad_gate_act, grad_up_act], axis=1)
    norm_two_grad = both(dot(grad_acts, mat_ffn, 1, 1))
    grad_down = reduce_rows(dot(cot, hidden, 0, 0).astype(BF)).T
    grad_ffn = reduce_rows(dot(normed_two, grad_acts, 0, 0).astype(BF))
    grad_postnorm = jnp.sum(norm_two_grad * resid_mid * scale_two, axis=0)
    grad_mid = cot.astype(F32) + norm_back(norm_two_grad, resid_mid, scale_two, gain_second)
    grad_attn = grad_mid.astype(BF)
    grad_gated = dot(grad_attn, mat_output, 1, 1)
    grad_output = reduce_rows(dot(grad_attn, gated, 0, 0).astype(BF)).T

    grad_mixed, grad_gate_rows, headnorm_part, adjoint = back_start_call(
        ids, prev_id, ids_col, query, total, gate_pre, gain_head, mixed, grad_gated
    )
    adjoint_all = lax.all_gather(adjoint.astype(BF), "ctx")
    adjoint_in = chain(
        columns, adjoint_all, range(pieces - 1, -1, -1), lambda source: source > place
    )
    grad_query, grad_key, grad_value, grad_log_decay = backward_call(
        ids, prev_id, ids_col, ids_row, query, key, value, total, grad_mixed, states, adjoint_in
    )
    grad_logit = (grad_log_decay * jax.nn.sigmoid(-decay_logit) / NORMALIZER).astype(BF)
    grad_decay = dot(rank_act, grad_logit, 0, 0)
    grad_bias = jnp.sum(grad_logit.astype(F32), axis=0, keepdims=True)
    grad_rank = both(dot(grad_logit, w_decay, 1, 1)).astype(BF)
    grad_heads = jnp.concatenate([grad_query, grad_key, grad_value, grad_gate_rows], axis=1)
    grad_mixer = dot(normed_one, grad_heads, 0, 0).astype(BF)
    grad_lowrank = dot(normed_one, grad_rank, 0, 0).astype(BF)
    norm_one_grad = both(dot(grad_heads, mixer_all[:, :mixer_size], 1, 1))
    norm_one_grad = norm_one_grad + dot(grad_rank, mat_lowrank, 1, 1)
    grad_prenorm = jnp.sum(norm_one_grad * resid_in * scale_one, axis=0)
    grad_tokens = (grad_mid + norm_back(norm_one_grad, resid_in, scale_one, gain_first)).astype(BF)
    grad_heads_own = reduce_rows(grad_mixer)
    grad_small = jnp.concatenate(
        [
            grad_lowrank,
            grad_prenorm[:, None].astype(BF),
            grad_postnorm[:, None].astype(BF),
            jnp.zeros((grad_lowrank.shape[0], extra), BF),
        ],
        axis=1,
    )
    small_own = reduce_rows(grad_small)
    sums = lax.psum(
        jnp.concatenate([grad_decay, grad_bias, both(headnorm_part)], axis=0), ("fsdp", "ctx")
    )
    return (
        block_out[None],
        grad_tokens[None],
        small_own[:, rank],
        grad_heads_own[:, :keys],
        grad_heads_own[:, keys : 2 * keys],
        grad_heads_own[:, 2 * keys : 2 * keys + values],
        grad_heads_own[:, 2 * keys + values :],
        small_own[:, :rank],
        sums[:rank],
        sums[rank],
        sums[rank + 1],
        grad_output,
        small_own[:, rank + 1],
        grad_ffn[:, :hidden_size],
        grad_ffn[:, hidden_size:],
        grad_down,
    )


def solution(mesh):
    in_specs = (
        P("fsdp", "ctx", None),
        P("fsdp", "ctx"),
        P("fsdp"),
        P("fsdp", "tp"),
        P("fsdp", "tp"),
        P("fsdp", "tp"),
        P("fsdp", "tp"),
        P("fsdp", None),
        P(None, "tp"),
        P("tp"),
        P(),
        P("tp", "fsdp"),
        P("fsdp"),
        P("fsdp", "tp"),
        P("fsdp", "tp"),
        P("tp", "fsdp"),
        P("fsdp", "ctx", None),
    )
    out_specs = (
        P("fsdp", "ctx", None),
        P("fsdp", "ctx", None),
        P("fsdp"),
        P("fsdp", "tp"),
        P("fsdp", "tp"),
        P("fsdp", "tp"),
        P("fsdp", "tp"),
        P("fsdp", None),
        P(None, "tp"),
        P("tp"),
        P(),
        P("tp", "fsdp"),
        P("fsdp"),
        P("fsdp", "tp"),
        P("fsdp", "tp"),
        P("tp", "fsdp"),
    )
    return jax.shard_map(body, mesh=mesh, in_specs=in_specs, out_specs=out_specs, check_vma=False)
```

time: 1310 us -> 697 us (0.53); the launches traced: 1290 us -> 692 us
  waiting for transfers between devices: 447 us -> 214 us
  matrix products: 268 us -> 73 us
  local copies, waits for them, and re-layouts: 193 us -> 80.2 us
  starting transfers between devices: 6.74 us -> 113 us
  blocking collectives: 191 us -> 94.5 us
  other arithmetic: 120 us -> 59.1 us
  loops' own time: 44.3 us -> 0 us
  Pallas kernels: 0 us -> 40.8 us
    reduce_scatter x9 -> x0, waiting for transfers between devices: 219 us -> none  [the longest x1 58.4 us: body(): lax.psum_scatter(grad_up.astype(jnp.bfloat16), 'fsdp', scatter_dimension=...]
    ppermute x0 -> x89, waiting for transfers between devices: none -> 199 us  [the longest x62 160 us: swap(): return lax.ppermute(array, axis, [(i, i ^ bit) for i in range(count)])]
    dot_general x241 -> x17, matrix products: 268 us -> 73 us  [dot(): lax.dot_general(left, right, (((left_dim,), (right_dim,)), ((), ())), pre...]
    all_gather x7 -> x1, waiting for transfers between devices: 157 us -> 14.7 us  [body(): ending_all = lax.all_gather(ending, 'ctx')]
    ppermute x0 -> x89, starting transfers between devices: none -> 109 us  [the longest x62 62.2 us: swap(): return lax.ppermute(array, axis, [(i, i ^ bit) for i in range(count)])]
    all_gather x8 -> x2, blocking collectives: 94.1 us -> 17.6 us  [the longest x1 9.1 us: body(): adjoint_all = lax.all_gather(adjoint.astype(BF), 'ctx')]
    squeeze x112 -> x11, local copies, waits for them, and re-layouts: 71 us -> 2.27 us  [pick(): return lax.dynamic_index_in_dim(array, index, axis, False)]
    psum x4 -> x0, waiting for transfers between devices: 67.3 us -> none  [the longest x1 36.9 us: body(): lax.psum(owned[1].astype(jnp.bfloat16), 'ctx').astype(jnp.float32)]
  transfers between devices with their start and end apart: 21 -> 91, of which waited for: 11 -> 49; matrix products, arithmetic and copies ran while one was open for 23% -> 21% of each run, Pallas kernels for 0% -> 6%
where the time goes in v1:
time: 697 us; the launch traced here: 692 us
  waiting for transfers between devices  214 us (31%)
  starting transfers between devices  113 us (16%)
  blocking collectives  94.5 us (14%)
  local copies, waits for them, and re-layouts  80.2 us (12%)
  matrix products  73 us (10%)
  other arithmetic  59.1 us (8%)
  Pallas kernels  40.8 us (6%)
  between operations  17.4 us (2%)
    ppermute x62, waiting for transfers between devices, swap(): return lax.ppermute(array, axis, [(i, i ^ bit) for i in range(count)])  160 us
    psum x1, blocking collectives, body(): lax.psum(jnp.concatenate([grad_decay, grad_bias, both(headnorm_part)], ax...  76.9 us
    dot_general x17, matrix products, dot(): lax.dot_general(left, right, (((left_dim,), (right_dim,)), ((), ())), pre...  73 us
    ppermute x62, starting transfers between devices, swap(): return lax.ppermute(array, axis, [(i, i ^ bit) for i in range(count)])  62.2 us
    pallas_call x4, Pallas kernels, call(): pl.pallas_call(kernel, out_shape=shapes, in_specs=[pl.BlockSpec(memory_sp...  40.8 us
    unnamed x136, local copies, waits for them, and re-layouts  31.6 us
    ppermute x15, waiting for transfers between devices, reduce_rows(): lax.ppermute(sent, 'fsdp', [(i, (i + shift) % count) for i in range(count)])  30.1 us
    ppermute x12, starting transfers between devices, gather_rows(): lax.ppermute(part, 'fsdp', [(i, (i + shift) % count) for i in range(count)])  26.5 us
  transfers between devices with their start and end apart: 91, of which 49 were waited for; matrix products, arithmetic and copies ran while one was open for 21% of the time, Pallas kernels for 6%

profile of v1, /device:TPU:0, one launch (start us, length us, event | category | flops | bytes accessed | tf_op | source)
XLA Modules:
  0.0 692.0 jit_solution(8966687373671023515)
XLA Ops:
  20.4 3.9 collective-permute-start
  36.7 4.0 copy.206
  48.8 7.1 %collective-permute-start.24 = (bf16[64,1408]{1,0:T(8,128)(2,1)S(1)}, bf16[64,1408]{1,0:T(8,128)(2,1)S(1)}, u32[]{:S(2)}, u32[]{:S(2)}) collective-permute-start(bf16[64,1408]{1,0:T(8,128)(2,1)S(1)} %bitcast.715), channel_id=1, source_target_pairs={{0,16},{8,24},{16,0},{24,8},{1,17},{9,25},{17,1},{25,9},{2,18},{10... | collective-permute-start | bytes 540680 | tf_op jit(solution)/shard_map/ppermute | solution.py:425
  57.5 3.5 collective-permute-start.25
  65.1 3.1 collective-permute-done.11
  71.6 3.3 collective-permute-start.18
  84.9 6.3 collective-permute-done.17
  111.6 9.6 %collective-permute-done.19 = bf16[2,64,2816]{2,1,0:T(8,128)(2,1)S(1)} collective-permute-done((bf16[2,64,2816]{2,1,0:T(8,128)(2,1)S(1)}, bf16[2,64,2816]{2,1,0:T(8,128)(2,1)S(1)}, u32[]{:S(2)}, u32[]{:S(2)}) %collective-permute-start.19) | collective-permute-done | bytes 720928 | tf_op jit(solution)/shard_map/ppermute | solution.py:376
  129.7 7.0 %collective-permute-done.29 = bf16[2,2,64,1408]{3,2,1,0:T(8,128)(2,1)S(1)} collective-permute-done((bf16[2,2,64,1408]{3,2,1,0:T(8,128)(2,1)S(1)}, bf16[2,2,64,1408]{3,2,1,0:T(8,128)(2,1)S(1)}, u32[]{:S(2)}, u32[]{:S(2)}) %collective-permute-start.29) | collective-permute-done | bytes 720928 | tf_op jit(solution)/shard_map/ppermute | solution.py:376
  141.5 15.7 %collective-permute-done.5 = bf16[2,2,64,1664]{3,2,0,1:T(8,128)(2,1)S(1)} collective-permute-done((bf16[2,2,64,1664]{3,2,0,1:T(8,128)(2,1)S(1)}, bf16[2,2,64,1664]{3,2,0,1:T(8,128)(2,1)S(1)}, u32[]{:S(2)}, u32[]{:S(2)}) %collective-permute-start.5) | collective-permute-done | bytes 852000 | tf_op jit(solution)/shard_map/ppermute | solution.py:376
  158.9 6.3 fusion.169
  168.1 6.4 shard_map.288
  179.2 3.2 slice.395.gate
  182.4 8.5 %all-gather.3 = f32[4,1,256]{2,1,0:T(1,128)S(1)} all-gather(f32[1,1,256]{2,1,0:T(1,128)S(1)} %multiply_bitcast_fusion), channel_id=2, replica_groups=mesh['fsdp'=4,'ctx'=4,'tp'=2] {'ctx'}, dimensions={0}, use_global_device_ids=true | all-gather | bytes 5120 | tf_op jit(solution)/shard_map/all_gather | solution.py:554
  194.0 14.7 %all-gather.6.cloned.1.call-done = f32[2048,128]{1,0:T(8,128)} async-done(((f32[512,128]{1,0:T(8,128)}), f32[2048,128]{1,0:T(8,128)}) %all-gather.6.cloned.1.call-update) | async-done | bytes 1048592 | tf_op jit(solution)/shard_map/all_gather | solution.py:555
  210.1 9.1 %shard_map.289 = (f32[1024,512]{1,0:T(8,128)}, bf16[1024,512]{1,0:T(8,128)(2,1)S(1)}, bf16[16,512,128]{2,1,0:T(8,128)(2,1)}) custom-call(s32[1024]{0:T(1024)S(1)} %bitcast.666, s32[1]{0:T(128)} %collective-permute-done.prev_s, s32[1024,1]{1,0:T(8,128)S(1)} %copy.193.ids_c, s32[16,64]{1,0:T(8,128)S(1)} %reshape_squeeze.3.ids_r, ...), custom_call_target="tpu_custom_call" | custom-call | flops 20000000000 | bytes 10761220 | tf_op jit(solution)/shard_map/pallas_call | solution.py:299
  230.9 9.4 %fusion.151 = f32[1024,2816]{1,0:T(8,128)} fusion(bf16[1024,2816]{1,0:T(8,128)(2,1)S(1)} %bitcast.682, f32[1024,1024]{0,1:T(8,128)S(1)} %get-tuple-element.119, f32[1024]{0:T(1024)S(1)} %get-tuple-element.112, f32[1024]{0:T(1024)S(1)} %add_rsqrt_fusion), kind=kOutput, calls=%fused_computation.456 | convolution fusion | flops 5908725760 | bytes 21504000 | tf_op jit(solution)/shard_map/dot_general | solution.py:472
  240.3 8.1 %fusion.2 = (bf16[1024,1408]{1,0:T(8,128)(2,1)S(1)}, bf16[1024,1408]{1,0:T(8,128)(2,1)S(1)}, bf16[1024,1408]{1,0:T(8,128)(2,1)S(1)}) fusion(f32[1024,2816]{1,0:T(8,128)} %fusion.151, bf16[1024,1408]{1,0:T(8,128)(2,1)S(1)} %bitcast.695, bf16[1,1024,1024]{2,1,0:T(8,128)(2,1)S(1)} %copy-done.34), kind=kOutput, calls=%fused_computation.6 | convolution fusion | flops 2974416896 | bytes 25165824 | tf_op jit(solution)/shard_map/dot_general | solution.py:472
  251.0 7.4 %fusion.44 = bf16[1024,1024]{0,1:T(8,128)(2,1)} fusion(bf16[1024,2816]{1,0:T(8,128)(2,1)S(1)} %bitcast.683, bf16[1024,1408]{1,0:T(8,128)(2,1)S(1)} %get-tuple-element.125, bf16[1024,1408]{1,0:T(8,128)(2,1)S(1)} %get-tuple-element.124), kind=kOutput, calls=%fused_computation.76 | convolution fusion | flops 5918162944 | bytes 13631488 | tf_op jit(solution)/shard_map/dot_general | solution.py:472
  258.4 9.7 %convolution_convert_fusion = bf16[1024,2816]{1,0:T(8,128)(2,1)S(1)} fusion(bf16[1024,1408]{1,0:T(8,128)(2,1)} %copy-done.60, bf16[1024,1408]{1,0:T(8,128)(2,1)} %copy-done.59, f32[1024,1024]{0,1:T(8,128)S(1)} %get-tuple-element.119, f32[1024]{0:T(1024)S(1)} %get-tuple-element.112, f32[1024]{0:T(1024)S(1)} %add_rsqrt_fusion), kind=kOutput, calls=%fused_computation.11 | convolution fusion | flops 5923143680 | bytes 15736832 | tf_op jit(solution)/shard_map/dot_general | solution.py:472
  268.1 4.7 convolution_convert_fusion.3
  272.7 3.7 fusion.26
  280.2 15.5 %collective-permute-done.79 = bf16[2,2,64,1408]{3,2,0,1:T(8,128)(2,1)S(1)} collective-permute-done((bf16[2,2,64,1408]{3,2,0,1:T(8,128)(2,1)S(1)}, bf16[2,2,64,1408]{3,2,0,1:T(8,128)(2,1)S(1)}, u32[]{:S(2)}, u32[]{:S(2)}) %collective-permute-start.79) | collective-permute-done | bytes 720928 | tf_op jit(solution)/shard_map/ppermute | solution.py:376
  298.3 7.2 %collective-permute-done.80 = bf16[2,64,1408]{2,1,0:T(8,128)(2,1)S(1)} collective-permute-done((bf16[2,64,1408]{2,1,0:T(8,128)(2,1)S(1)}, bf16[2,64,1408]{2,1,0:T(8,128)(2,1)S(1)}, u32[]{:S(2)}, u32[]{:S(2)}) %collective-permute-start.80) | collective-permute-done | bytes 360480 | tf_op jit(solution)/shard_map/ppermute | solution.py:376
  307.3 3.4 collective-permute-start.85
  312.3 3.4 collective-permute-done.85
  316.3 9.0 %collective-permute-done.84 = bf16[64,1408]{1,0:T(8,128)(2,1)S(1)} collective-permute-done((bf16[64,1408]{1,0:T(8,128)(2,1)S(1)}, bf16[64,1408]{1,0:T(8,128)(2,1)S(1)}, u32[]{:S(2)}, u32[]{:S(2)}) %collective-permute-start.84) | collective-permute-done | bytes 180256 | tf_op jit(solution)/shard_map/ppermute | solution.py:457
  327.9 20.4 %collective-permute-done.86 = bf16[1,32,1408]{2,1,0:T(8,128)(2,1)S(1)} collective-permute-done((bf16[1,32,1408]{2,1,0:T(8,128)(2,1)S(1)}, bf16[1,32,1408]{2,1,0:T(8,128)(2,1)S(1)}, u32[]{:S(2)}, u32[]{:S(2)}) %collective-permute-start.86) | collective-permute-done | bytes 90144 | tf_op jit(solution)/shard_map/ppermute | solution.py:376
  352.3 30.5 %collective-permute-done.70 = bf16[2,2,64,2816]{3,2,0,1:T(8,128)(2,1)S(1)} collective-permute-done((bf16[2,2,64,2816]{3,2,0,1:T(8,128)(2,1)S(1)}, bf16[2,2,64,2816]{3,2,0,1:T(8,128)(2,1)S(1)}, u32[]{:S(2)}, u32[]{:S(2)}) %collective-permute-start.70) | collective-permute-done | bytes 1441824 | tf_op jit(solution)/shard_map/ppermute | solution.py:376
  388.2 5.0 multiply_reduce_fusion
  393.5 6.6 multiply_add_fusion
  402.8 7.7 %shard_map.290 = (bf16[1024,512]{1,0:T(8,128)(2,1)S(1)}, bf16[1024,512]{1,0:T(8,128)(2,1)S(1)}, f32[1,256]{1,0:T(1,128)S(1)}, f32[512,128]{1,0:T(8,128)S(1)}) custom-call(s32[1024]{0:T(1024)S(1)} %bitcast.667, s32[1]{0:T(128)} %collective-permute-done.prev_s, s32[1024,1]{1,0:T(8,128)S(1)} %copy.193.ids_c, bf16[1024,256]{1,0:T(8,128)(2,1)S(1)} %get-tuple-element.132.query, ...), custom_call_target="tpu_custom_call" | custom-call | flops 15000000512 | bytes 10233860 | tf_op jit(solution)/shard_map/pallas_call | solution.py:299
  411.5 9.1 %all-gather.2 = bf16[2048,128]{1,0:T(8,128)(2,1)S(1)} all-gather(bf16[512,128]{1,0:T(8,128)(2,1)S(1)} %convert_element_type.606), channel_id=4, replica_groups=mesh['fsdp'=4,'ctx'=4,'tp'=2] {'ctx'}, dimensions={0}, use_global_device_ids=true | all-gather | bytes 655360 | tf_op jit(solution)/shard_map/all_gather | solution.py:589
  420.7 17.7 %shard_map.291 = (bf16[1024,256]{1,0:T(8,128)(2,1)S(1)}, bf16[1024,256]{1,0:T(8,128)(2,1)S(1)}, bf16[1024,512]{1,0:T(8,128)(2,1)S(1)}, f32[1024,256]{1,0:T(8,128)}) custom-call(s32[1024]{0:T(1024)S(1)} %bitcast.668, s32[1]{0:T(128)} %collective-permute-done.prev_s, s32[1024,1]{1,0:T(8,128)S(1)} %copy.193.ids_c, s32[16,64]{1,0:T(8,128)S(1)} %reshape_squeeze.3.ids_r, ...), custom_call_target="tpu_custom_call" | custom-call | flops 40000000000 | bytes 9711620 | tf_op jit(solution)/shard_map/pallas_call | solution.py:299
  440.4 4.6 fusion.41
  445.1 5.0 convolution_convert_fusion.2
  454.3 3.9 copy.244
  469.0 76.9 %psum.7 = f32[18,256]{1,0:T(8,128)S(1)} all-reduce(f32[18,256]{1,0:T(8,128)S(1)} %pad_maximum_fusion.43), channel_id=1, replica_groups=mesh['fsdp'=4,'ctx'=4,'tp'=2] {'fsdp','ctx'}, use_global_device_ids=true, to_apply=%region_7.8 | all-reduce | flops 4608 | bytes 36864 | tf_op jit(solution)/shard_map/psum | solution.py:618
  560.4 4.9 collective-permute-done.60
  568.2 3.5 collective-permute-done.73
  582.6 5.7 collective-permute-done.66
  588.4 4.2 collective-permute-done.67
  594.4 3.3 collective-permute-done.65
  613.2 4.0 collective-permute-done.46
  620.9 3.8 collective-permute-start.50
  626.9 7.8 %collective-permute-done.50 = bf16[64,1536]{1,0:T(8,128)(2,1)S(1)} collective-permute-done((bf16[64,1536]{1,0:T(8,128)(2,1)S(1)}, bf16[64,1536]{1,0:T(8,128)(2,1)S(1)}, u32[]{:S(2)}, u32[]{:S(2)}) %collective-permute-start.50) | collective-permute-done | bytes 196640 | tf_op jit(solution)/shard_map/ppermute | solution.py:457
  649.6 3.5 fusion.21
  679.4 3.9 copy.245
  (516 shorter events, 249.3 us)
Async XLA Ops:
  7.2 201.5 %all-gather.6.cloned.1.call-start = ((), (), s32[]{:S(2)}) async-start(), calls=%async_computation | async-start | bytes 1310720 | tf_op jit(solution)/shard_map/all_gather | solution.py:555
  12.8 58.8 %collective-permute-start.1 = (bf16[64,1664]{1,0:T(8,128)(2,1)}, bf16[64,1664]{1,0:T(8,128)(2,1)}, u32[]{:S(2)}, u32[]{:S(2)}) collective-permute-start(bf16[64,1664]{1,0:T(8,128)(2,1)} %get-tuple-element.123), channel_id=1, source_target_pairs={{0,8},{8,16},{16,24},{24,0},{1,9},{9,17},{17,25},{25,1},{2,10},{10... | collective-permute-start | bytes 638984 | tf_op jit(solution)/shard_map/ppermute | solution.py:425
  15.8 60.7 %collective-permute-start.2 = (bf16[64,1664]{1,0:T(8,128)(2,1)}, bf16[64,1664]{1,0:T(8,128)(2,1)}, u32[]{:S(2)}, u32[]{:S(2)}) collective-permute-start(bf16[64,1664]{1,0:T(8,128)(2,1)} %get-tuple-element.123), channel_id=1, source_target_pairs={{0,16},{8,24},{16,0},{24,8},{1,17},{9,25},{17,1},{25,9},{2,18},{10... | collective-permute-start | bytes 638984 | tf_op jit(solution)/shard_map/ppermute | solution.py:425
  18.4 60.8 %collective-permute-start.3 = (bf16[64,1664]{1,0:T(8,128)(2,1)}, bf16[64,1664]{1,0:T(8,128)(2,1)}, u32[]{:S(2)}, u32[]{:S(2)}) collective-permute-start(bf16[64,1664]{1,0:T(8,128)(2,1)} %get-tuple-element.123), channel_id=1, source_target_pairs={{0,24},{8,0},{16,8},{24,16},{1,25},{9,1},{17,9},{25,17},{2,26},{10... | collective-permute-start | bytes 638984 | tf_op jit(solution)/shard_map/ppermute | solution.py:425
  20.4 20.9 %collective-permute-start = (s32[1]{0:T(128)}, s32[1]{0:T(128)}, u32[]{:S(2)}, u32[]{:S(2)}) collective-permute-start(s32[1]{0:T(128)} %bitcast.2), channel_id=1, source_target_pairs={{0,2},{2,4},{4,6},{1,3},{3,5},{5,7},{8,10},{10,12},{12,14},{9,11},... | collective-permute-start | bytes 20 | tf_op jit(solution)/shard_map/ppermute | solution.py:468
  25.1 17.8 %collective-permute-start.8 = (bf16[64,512]{1,0:T(8,128)(2,1)}, bf16[64,512]{1,0:T(8,128)(2,1)}, u32[]{:S(2)}, u32[]{:S(2)}) collective-permute-start(bf16[64,512]{1,0:T(8,128)(2,1)} %bitcast.33), channel_id=1, source_target_pairs={{0,8},{8,16},{16,24},{24,0},{1,9},{9,17},{17,25},{25,1},{2,10},{10... | collective-permute-start | bytes 196616 | tf_op jit(solution)/shard_map/ppermute | solution.py:425
  48.8 14.5 %collective-permute-start.24 = (bf16[64,1408]{1,0:T(8,128)(2,1)S(1)}, bf16[64,1408]{1,0:T(8,128)(2,1)S(1)}, u32[]{:S(2)}, u32[]{:S(2)}) collective-permute-start(bf16[64,1408]{1,0:T(8,128)(2,1)S(1)} %bitcast.715), channel_id=1, source_target_pairs={{0,16},{8,24},{16,0},{24,8},{1,17},{9,25},{17,1},{25,9},{2,18},{10... | collective-permute-start | bytes 540680 | tf_op jit(solution)/shard_map/ppermute | solution.py:425
  68.3 13.8 %collective-permute-start.16 = (bf16[64,2816]{1,0:T(8,128)(2,1)S(1)}, bf16[64,2816]{1,0:T(8,128)(2,1)S(1)}, u32[]{:S(2)}, u32[]{:S(2)}) collective-permute-start(bf16[64,2816]{1,0:T(8,128)(2,1)S(1)} %copy-done.41), channel_id=1, source_target_pairs={{0,8},{8,16},{16,24},{24,0},{1,9},{9,17},{17,25},{25,1},{2,10},{10... | collective-permute-start | bytes 1081352 | tf_op jit(solution)/shard_map/ppermute | solution.py:425
  69.4 21.9 %collective-permute-start.17 = (bf16[64,2816]{1,0:T(8,128)(2,1)S(1)}, bf16[64,2816]{1,0:T(8,128)(2,1)S(1)}, u32[]{:S(2)}, u32[]{:S(2)}) collective-permute-start(bf16[64,2816]{1,0:T(8,128)(2,1)S(1)} %copy-done.41), channel_id=1, source_target_pairs={{0,16},{8,24},{16,0},{24,8},{1,17},{9,25},{17,1},{25,9},{2,18},{10... | collective-permute-start | bytes 1081352 | tf_op jit(solution)/shard_map/ppermute | solution.py:425
  71.6 21.4 %collective-permute-start.18 = (bf16[64,2816]{1,0:T(8,128)(2,1)S(1)}, bf16[64,2816]{1,0:T(8,128)(2,1)S(1)}, u32[]{:S(2)}, u32[]{:S(2)}) collective-permute-start(bf16[64,2816]{1,0:T(8,128)(2,1)S(1)} %copy-done.41), channel_id=1, source_target_pairs={{0,24},{8,0},{16,8},{24,16},{1,25},{9,1},{17,9},{25,17},{2,26},{10... | collective-permute-start | bytes 1081352 | tf_op jit(solution)/shard_map/ppermute | solution.py:425
  76.6 24.5 %collective-permute-start.26 = (bf16[2,64,1408]{2,1,0:T(8,128)(2,1)S(1)}, bf16[2,64,1408]{2,1,0:T(8,128)(2,1)S(1)}, u32[]{:S(2)}, u32[]{:S(2)}) collective-permute-start(bf16[2,64,1408]{2,1,0:T(8,128)(2,1)S(1)} %get-tuple-element.204), channel_id=1, source_target_pairs={{0,2},{2,0},{4,6},{6,4},{1,3},{3,1},{5,7},{7,5},{8,10},{10,8},{12,... | collective-permute-start | bytes 1081352 | tf_op jit(solution)/shard_map/ppermute | solution.py:376
  79.2 23.5 %collective-permute-start.28 = (bf16[2,64,1408]{2,1,0:T(8,128)(2,1)S(1)}, bf16[2,64,1408]{2,1,0:T(8,128)(2,1)S(1)}, u32[]{:S(2)}, u32[]{:S(2)}) collective-permute-start(bf16[2,64,1408]{2,1,0:T(8,128)(2,1)S(1)} %get-tuple-element.205), channel_id=1, source_target_pairs={{0,4},{2,6},{4,0},{6,2},{1,5},{3,7},{5,1},{7,3},{8,12},{10,14},{12... | collective-permute-start | bytes 1081352 | tf_op jit(solution)/shard_map/ppermute | solution.py:376
  82.1 13.2 %collective-permute-start.14 = (bf16[2,2,64,512]{3,2,1,0:T(8,128)(2,1)S(1)}, bf16[2,2,64,512]{3,2,1,0:T(8,128)(2,1)S(1)}, u32[]{:S(2)}, u32[]{:S(2)}) collective-permute-start(bf16[2,2,64,512]{3,2,1,0:T(8,128)(2,1)S(1)} %pad_maximum_fusion.32), channel_id=1, source_target_pairs={{0,2},{2,0},{4,6},{6,4},{1,3},{3,1},{5,7},{7,5},{8,10},{10,8},{12,... | collective-permute-start | bytes 786440 | tf_op jit(solution)/shard_map/ppermute | solution.py:376
  93.0 12.8 %collective-permute-start.4 = (bf16[2,64,1664]{2,1,0:T(8,128)(2,1)S(1)}, bf16[2,64,1664]{2,1,0:T(8,128)(2,1)S(1)}, u32[]{:S(2)}, u32[]{:S(2)}) collective-permute-start(bf16[2,64,1664]{2,1,0:T(8,128)(2,1)S(1)} %get-tuple-element.190), channel_id=1, source_target_pairs={{0,2},{2,0},{4,6},{6,4},{1,3},{3,1},{5,7},{7,5},{8,10},{10,8},{12,... | collective-permute-start | bytes 1277960 | tf_op jit(solution)/shard_map/ppermute | solution.py:376
  95.3 12.8 %collective-permute-start.6 = (bf16[2,64,1664]{2,1,0:T(8,128)(2,1)S(1)}, bf16[2,64,1664]{2,1,0:T(8,128)(2,1)S(1)}, u32[]{:S(2)}, u32[]{:S(2)}) collective-permute-start(bf16[2,64,1664]{2,1,0:T(8,128)(2,1)S(1)} %get-tuple-element.191), channel_id=1, source_target_pairs={{0,4},{2,6},{4,0},{6,2},{1,5},{3,7},{5,1},{7,3},{8,12},{10,14},{12... | collective-permute-start | bytes 1277960 | tf_op jit(solution)/shard_map/ppermute | solution.py:376
  98.6 22.6 %collective-permute-start.19 = (bf16[2,64,2816]{2,1,0:T(8,128)(2,1)S(1)}, bf16[2,64,2816]{2,1,0:T(8,128)(2,1)S(1)}, u32[]{:S(2)}, u32[]{:S(2)}) collective-permute-start(bf16[2,64,2816]{2,1,0:T(8,128)(2,1)S(1)} %get-tuple-element.176), channel_id=1, source_target_pairs={{0,2},{2,0},{4,6},{6,4},{1,3},{3,1},{5,7},{7,5},{8,10},{10,8},{12,... | collective-permute-start | bytes 2162696 | tf_op jit(solution)/shard_map/ppermute | solution.py:376
  101.1 22.4 %collective-permute-start.21 = (bf16[2,64,2816]{2,1,0:T(8,128)(2,1)S(1)}, bf16[2,64,2816]{2,1,0:T(8,128)(2,1)S(1)}, u32[]{:S(2)}, u32[]{:S(2)}) collective-permute-start(bf16[2,64,2816]{2,1,0:T(8,128)(2,1)S(1)} %get-tuple-element.177), channel_id=1, source_target_pairs={{0,4},{2,6},{4,0},{6,2},{1,5},{3,7},{5,1},{7,3},{8,12},{10,14},{12... | collective-permute-start | bytes 2162696 | tf_op jit(solution)/shard_map/ppermute | solution.py:376
  102.9 33.8 %collective-permute-start.29 = (bf16[2,2,64,1408]{3,2,1,0:T(8,128)(2,1)S(1)}, bf16[2,2,64,1408]{3,2,1,0:T(8,128)(2,1)S(1)}, u32[]{:S(2)}, u32[]{:S(2)}) collective-permute-start(bf16[2,2,64,1408]{3,2,1,0:T(8,128)(2,1)S(1)} %pad_maximum_fusion.20), channel_id=1, source_target_pairs={{0,2},{2,0},{4,6},{6,4},{1,3},{3,1},{5,7},{7,5},{8,10},{10,8},{12,... | collective-permute-start | bytes 2162696 | tf_op jit(solution)/shard_map/ppermute | solution.py:376
  105.8 33.2 %collective-permute-start.27 = (bf16[2,2,64,1408]{3,2,0,1:T(8,128)(2,1)S(1)}, bf16[2,2,64,1408]{3,2,0,1:T(8,128)(2,1)S(1)}, u32[]{:S(2)}, u32[]{:S(2)}) collective-permute-start(bf16[2,2,64,1408]{3,2,0,1:T(8,128)(2,1)S(1)} %pad_maximum_fusion.19), channel_id=1, source_target_pairs={{0,4},{2,6},{4,0},{6,2},{1,5},{3,7},{5,1},{7,3},{8,12},{10,14},{12... | collective-permute-start | bytes 2162696 | tf_op jit(solution)/shard_map/ppermute | solution.py:376
  109.5 48.2 %collective-permute-start.7 = (bf16[2,2,64,1664]{3,2,1,0:T(8,128)(2,1)S(1)}, bf16[2,2,64,1664]{3,2,1,0:T(8,128)(2,1)S(1)}, u32[]{:S(2)}, u32[]{:S(2)}) collective-permute-start(bf16[2,2,64,1664]{3,2,1,0:T(8,128)(2,1)S(1)} %pad_maximum_fusion.18), channel_id=1, source_target_pairs={{0,2},{2,0},{4,6},{6,4},{1,3},{3,1},{5,7},{7,5},{8,10},{10,8},{12,... | collective-permute-start | bytes 2555912 | tf_op jit(solution)/shard_map/ppermute | solution.py:376
  121.2 36.1 %collective-permute-start.5 = (bf16[2,2,64,1664]{3,2,0,1:T(8,128)(2,1)S(1)}, bf16[2,2,64,1664]{3,2,0,1:T(8,128)(2,1)S(1)}, u32[]{:S(2)}, u32[]{:S(2)}) collective-permute-start(bf16[2,2,64,1664]{3,2,0,1:T(8,128)(2,1)S(1)} %pad_maximum_fusion.17), channel_id=1, source_target_pairs={{0,4},{2,6},{4,0},{6,2},{1,5},{3,7},{5,1},{7,3},{8,12},{10,14},{12... | collective-permute-start | bytes 2555912 | tf_op jit(solution)/shard_map/ppermute | solution.py:376
  126.5 95.3 %collective-permute-start.22 = (bf16[2,2,64,2816]{3,2,1,0:T(8,128)(2,1)}, bf16[2,2,64,2816]{3,2,1,0:T(8,128)(2,1)}, u32[]{:S(2)}, u32[]{:S(2)}) collective-permute-start(bf16[2,2,64,2816]{3,2,1,0:T(8,128)(2,1)} %pad_maximum_fusion.13), channel_id=1, source_target_pairs={{0,2},{2,0},{4,6},{6,4},{1,3},{3,1},{5,7},{7,5},{8,10},{10,8},{12,... | collective-permute-start | bytes 4325384 | tf_op jit(solution)/shard_map/ppermute | solution.py:376
  136.6 54.2 %collective-permute-start.20 = (bf16[2,2,64,2816]{3,2,0,1:T(8,128)(2,1)}, bf16[2,2,64,2816]{3,2,0,1:T(8,128)(2,1)}, u32[]{:S(2)}, u32[]{:S(2)}) collective-permute-start(bf16[2,2,64,2816]{3,2,0,1:T(8,128)(2,1)} %pad_maximum_fusion.12), channel_id=1, source_target_pairs={{0,4},{2,6},{4,0},{6,2},{1,5},{3,7},{5,1},{7,3},{8,12},{10,14},{12... | collective-permute-start | bytes 4325384 | tf_op jit(solution)/shard_map/ppermute | solution.py:376
  276.5 111.7 %collective-permute-start.31 = (bf16[1024,1024]{0,1:T(8,128)(2,1)}, bf16[1024,1024]{0,1:T(8,128)(2,1)}, u32[]{:S(2)}, u32[]{:S(2)}) collective-permute-start(bf16[1024,1024]{0,1:T(8,128)(2,1)} %fusion.44), channel_id=1, source_target_pairs={{0,1},{1,0},{2,3},{3,2},{4,5},{5,4},{6,7},{7,6},{8,9},{9,8},{10,11... | collective-permute-start | bytes 6291464 | tf_op jit(solution)/shard_map/ppermute | solution.py:376
  276.6 116.6 %collective-permute-start.30 = (bf16[1024,1024]{0,1:T(8,128)(2,1)}, bf16[1024,1024]{0,1:T(8,128)(2,1)}, u32[]{:S(2)}, u32[]{:S(2)}) collective-permute-start(bf16[1024,1024]{0,1:T(8,128)(2,1)} %convolution_convert_fusion.3), channel_id=1, source_target_pairs={{0,1},{1,0},{2,3},{3,2},{4,5},{5,4},{6,7},{7,6},{8,9},{9,8},{10,11... | collective-permute-start | bytes 6291464 | tf_op jit(solution)/shard_map/ppermute | solution.py:376
  277.5 18.2 %collective-permute-start.79 = (bf16[2,2,64,1408]{3,2,0,1:T(8,128)(2,1)S(1)}, bf16[2,2,64,1408]{3,2,0,1:T(8,128)(2,1)S(1)}, u32[]{:S(2)}, u32[]{:S(2)}) collective-permute-start(bf16[2,2,64,1408]{3,2,0,1:T(8,128)(2,1)S(1)} %bitcast.713), channel_id=1, source_target_pairs={{0,2},{2,0},{4,6},{6,4},{1,3},{3,1},{5,7},{7,5},{8,10},{10,8},{12,... | collective-permute-start | bytes 2162696 | tf_op jit(solution)/shard_map/ppermute | solution.py:376
  279.2 18.2 %collective-permute-start.81 = (bf16[2,2,64,1408]{3,2,0,1:T(8,128)(2,1)S(1)}, bf16[2,2,64,1408]{3,2,0,1:T(8,128)(2,1)S(1)}, u32[]{:S(2)}, u32[]{:S(2)}) collective-permute-start(bf16[2,2,64,1408]{3,2,0,1:T(8,128)(2,1)S(1)} %bitcast.712), channel_id=1, source_target_pairs={{0,4},{2,6},{4,0},{6,2},{1,5},{3,7},{5,1},{7,3},{8,12},{10,14},{12... | collective-permute-start | bytes 2162696 | tf_op jit(solution)/shard_map/ppermute | solution.py:376
  310.7 14.6 %collective-permute-start.84 = (bf16[64,1408]{1,0:T(8,128)(2,1)S(1)}, bf16[64,1408]{1,0:T(8,128)(2,1)S(1)}, u32[]{:S(2)}, u32[]{:S(2)}) collective-permute-start(bf16[64,1408]{1,0:T(8,128)(2,1)S(1)} %get-tuple-element.196), channel_id=1, source_target_pairs={{0,16},{8,24},{16,0},{24,8},{1,17},{9,25},{17,1},{25,9},{2,18},{10... | collective-permute-start | bytes 540680 | tf_op jit(solution)/shard_map/ppermute | solution.py:457
  310.7 14.6 %collective-permute-start.83 = (bf16[64,1408]{1,0:T(8,128)(2,1)S(1)}, bf16[64,1408]{1,0:T(8,128)(2,1)S(1)}, u32[]{:S(2)}, u32[]{:S(2)}) collective-permute-start(bf16[64,1408]{1,0:T(8,128)(2,1)S(1)} %get-tuple-element.195), channel_id=1, source_target_pairs={{0,8},{8,16},{16,24},{24,0},{1,9},{9,17},{17,25},{25,1},{2,10},{10... | collective-permute-start | bytes 540680 | tf_op jit(solution)/shard_map/ppermute | solution.py:457
  315.7 34.8 %collective-permute-start.68 = (bf16[2,2,64,2816]{3,2,0,1:T(8,128)(2,1)S(1)}, bf16[2,2,64,2816]{3,2,0,1:T(8,128)(2,1)S(1)}, u32[]{:S(2)}, u32[]{:S(2)}) collective-permute-start(bf16[2,2,64,2816]{3,2,0,1:T(8,128)(2,1)S(1)} %bitcast.708), channel_id=1, source_target_pairs={{0,2},{2,0},{4,6},{6,4},{1,3},{3,1},{5,7},{7,5},{8,10},{10,8},{12,... | collective-permute-start | bytes 4325384 | tf_op jit(solution)/shard_map/ppermute | solution.py:376
  325.5 22.8 %collective-permute-start.86 = (bf16[1,32,1408]{2,1,0:T(8,128)(2,1)S(1)}, bf16[1,32,1408]{2,1,0:T(8,128)(2,1)S(1)}, u32[]{:S(2)}, u32[]{:S(2)}) collective-permute-start(bf16[1,32,1408]{2,1,0:T(8,128)(2,1)S(1)} %get-tuple-element.257), channel_id=1, source_target_pairs={{0,2},{2,0},{4,6},{6,4},{1,3},{3,1},{5,7},{7,5},{8,10},{10,8},{12,... | collective-permute-start | bytes 270344 | tf_op jit(solution)/shard_map/ppermute | solution.py:376
  326.1 22.5 %collective-permute-start.88 = (bf16[1,32,1408]{2,1,0:T(8,128)(2,1)S(1)}, bf16[1,32,1408]{2,1,0:T(8,128)(2,1)S(1)}, u32[]{:S(2)}, u32[]{:S(2)}) collective-permute-start(bf16[1,32,1408]{2,1,0:T(8,128)(2,1)S(1)} %get-tuple-element.258), channel_id=1, source_target_pairs={{0,4},{2,6},{4,0},{6,2},{1,5},{3,7},{5,1},{7,3},{8,12},{10,14},{12... | collective-permute-start | bytes 270344 | tf_op jit(solution)/shard_map/ppermute | solution.py:376
  348.3 34.5 %collective-permute-start.70 = (bf16[2,2,64,2816]{3,2,0,1:T(8,128)(2,1)S(1)}, bf16[2,2,64,2816]{3,2,0,1:T(8,128)(2,1)S(1)}, u32[]{:S(2)}, u32[]{:S(2)}) collective-permute-start(bf16[2,2,64,2816]{3,2,0,1:T(8,128)(2,1)S(1)} %bitcast.709), channel_id=1, source_target_pairs={{0,4},{2,6},{4,0},{6,2},{1,5},{3,7},{5,1},{7,3},{8,12},{10,14},{12... | collective-permute-start | bytes 4325384 | tf_op jit(solution)/shard_map/ppermute | solution.py:376
  348.7 35.8 %collective-permute-start.89 = (bf16[1,2,32,1408]{3,2,1,0:T(8,128)(2,1)S(1)}, bf16[1,2,32,1408]{3,2,1,0:T(8,128)(2,1)S(1)}, u32[]{:S(2)}, u32[]{:S(2)}) collective-permute-start(bf16[1,2,32,1408]{3,2,1,0:T(8,128)(2,1)S(1)} %pad_maximum_fusion.36), channel_id=1, source_target_pairs={{0,2},{2,0},{4,6},{6,4},{1,3},{3,1},{5,7},{7,5},{8,10},{10,8},{12,... | collective-permute-start | bytes 540680 | tf_op jit(solution)/shard_map/ppermute | solution.py:376
  350.5 35.8 %collective-permute-start.87 = (bf16[1,2,32,1408]{3,2,1,0:T(8,128)(2,1)S(1)}, bf16[1,2,32,1408]{3,2,1,0:T(8,128)(2,1)S(1)}, u32[]{:S(2)}, u32[]{:S(2)}) collective-permute-start(bf16[1,2,32,1408]{3,2,1,0:T(8,128)(2,1)S(1)} %pad_maximum_fusion.35), channel_id=1, source_target_pairs={{0,4},{2,6},{4,0},{6,2},{1,5},{3,7},{5,1},{7,3},{8,12},{10,14},{12... | collective-permute-start | bytes 540680 | tf_op jit(solution)/shard_map/ppermute | solution.py:376
  382.8 165.9 %collective-permute-start.69 = (bf16[2,64,2816]{2,1,0:T(8,128)(2,1)}, bf16[2,64,2816]{2,1,0:T(8,128)(2,1)}, u32[]{:S(2)}, u32[]{:S(2)}) collective-permute-start(bf16[2,64,2816]{2,1,0:T(8,128)(2,1)} %dynamic-slice_bitcast_fusion.1), channel_id=1, source_target_pairs={{0,4},{2,6},{4,0},{6,2},{1,5},{3,7},{5,1},{7,3},{8,12},{10,14},{12... | collective-permute-start | bytes 2162696 | tf_op jit(solution)/shard_map/ppermute | solution.py:376
  384.5 165.7 %collective-permute-start.71 = (bf16[2,64,2816]{2,1,0:T(8,128)(2,1)}, bf16[2,64,2816]{2,1,0:T(8,128)(2,1)}, u32[]{:S(2)}, u32[]{:S(2)}) collective-permute-start(bf16[2,64,2816]{2,1,0:T(8,128)(2,1)} %dynamic-slice_bitcast_fusion), channel_id=1, source_target_pairs={{0,2},{2,0},{4,6},{6,4},{1,3},{3,1},{5,7},{7,5},{8,10},{10,8},{12,... | collective-permute-start | bytes 2162696 | tf_op jit(solution)/shard_map/ppermute | solution.py:376
  458.2 88.9 %collective-permute-start.33 = (bf16[1024,16]{0,1:T(8,128)(2,1)S(1)}, bf16[1024,16]{0,1:T(8,128)(2,1)S(1)}, u32[]{:S(2)}, u32[]{:S(2)}) collective-permute-start(bf16[1024,16]{0,1:T(8,128)(2,1)S(1)} %convolution_convert_fusion.7), channel_id=1, source_target_pairs={{0,1},{1,0},{2,3},{3,2},{4,5},{5,4},{6,7},{7,6},{8,9},{9,8},{10,11... | collective-permute-start | bytes 98312 | tf_op jit(solution)/shard_map/ppermute | solution.py:376
  458.2 190.6 %collective-permute-start.32 = (bf16[1024,1024]{0,1:T(8,128)(2,1)}, bf16[1024,1024]{0,1:T(8,128)(2,1)}, u32[]{:S(2)}, u32[]{:S(2)}) collective-permute-start(bf16[1024,1024]{0,1:T(8,128)(2,1)} %fusion.41), channel_id=1, source_target_pairs={{0,1},{1,0},{2,3},{3,2},{4,5},{5,4},{6,7},{7,6},{8,9},{9,8},{10,11... | collective-permute-start | bytes 6291464 | tf_op jit(solution)/shard_map/ppermute | solution.py:376
  467.3 85.0 %collective-permute-start.57 = (bf16[2,2,64,512]{3,2,0,1:T(8,128)(2,1)}, bf16[2,2,64,512]{3,2,0,1:T(8,128)(2,1)}, u32[]{:S(2)}, u32[]{:S(2)}) collective-permute-start(bf16[2,2,64,512]{3,2,0,1:T(8,128)(2,1)} %bitcast.661), channel_id=1, source_target_pairs={{0,2},{2,0},{4,6},{6,4},{1,3},{3,1},{5,7},{7,5},{8,10},{10,8},{12,... | collective-permute-start | bytes 786440 | tf_op jit(solution)/shard_map/ppermute | solution.py:376
  552.2 13.3 %collective-permute-start.74 = (bf16[64,2816]{1,0:T(8,128)(2,1)S(1)}, bf16[64,2816]{1,0:T(8,128)(2,1)S(1)}, u32[]{:S(2)}, u32[]{:S(2)}) collective-permute-start(bf16[64,2816]{1,0:T(8,128)(2,1)S(1)} %get-tuple-element.169), channel_id=1, source_target_pairs={{0,24},{8,0},{16,8},{24,16},{1,25},{9,1},{17,9},{25,17},{2,26},{10... | collective-permute-start | bytes 1081352 | tf_op jit(solution)/shard_map/ppermute | solution.py:457
  552.2 19.4 %collective-permute-start.73 = (bf16[64,2816]{1,0:T(8,128)(2,1)S(1)}, bf16[64,2816]{1,0:T(8,128)(2,1)S(1)}, u32[]{:S(2)}, u32[]{:S(2)}) collective-permute-start(bf16[64,2816]{1,0:T(8,128)(2,1)S(1)} %get-tuple-element.168), channel_id=1, source_target_pairs={{0,16},{8,24},{16,0},{24,8},{1,17},{9,25},{17,1},{25,9},{2,18},{10... | collective-permute-start | bytes 1081352 | tf_op jit(solution)/shard_map/ppermute | solution.py:457
  552.3 19.3 %collective-permute-start.72 = (bf16[64,2816]{1,0:T(8,128)(2,1)S(1)}, bf16[64,2816]{1,0:T(8,128)(2,1)S(1)}, u32[]{:S(2)}, u32[]{:S(2)}) collective-permute-start(bf16[64,2816]{1,0:T(8,128)(2,1)S(1)} %get-tuple-element.167), channel_id=1, source_target_pairs={{0,8},{8,16},{16,24},{24,0},{1,9},{9,17},{17,25},{25,1},{2,10},{10... | collective-permute-start | bytes 1081352 | tf_op jit(solution)/shard_map/ppermute | solution.py:457
  565.3 42.0 %collective-permute-start.45 = (bf16[2,2,64,1536]{3,2,0,1:T(8,128)(2,1)}, bf16[2,2,64,1536]{3,2,0,1:T(8,128)(2,1)}, u32[]{:S(2)}, u32[]{:S(2)}) collective-permute-start(bf16[2,2,64,1536]{3,2,0,1:T(8,128)(2,1)} %bitcast.657), channel_id=1, source_target_pairs={{0,2},{2,0},{4,6},{6,4},{1,3},{3,1},{5,7},{7,5},{8,10},{10,8},{12,... | collective-permute-start | bytes 2359304 | tf_op jit(solution)/shard_map/ppermute | solution.py:376
  575.0 34.3 %collective-permute-start.47 = (bf16[2,2,64,1536]{3,2,0,1:T(8,128)(2,1)}, bf16[2,2,64,1536]{3,2,0,1:T(8,128)(2,1)}, u32[]{:S(2)}, u32[]{:S(2)}) collective-permute-start(bf16[2,2,64,1536]{3,2,0,1:T(8,128)(2,1)} %bitcast.656), channel_id=1, source_target_pairs={{0,4},{2,6},{4,0},{6,2},{1,5},{3,7},{5,1},{7,3},{8,12},{10,14},{12... | collective-permute-start | bytes 2359304 | tf_op jit(solution)/shard_map/ppermute | solution.py:376
  582.0 20.4 %collective-permute-start.75 = (bf16[1,32,2816]{2,1,0:T(8,128)(2,1)}, bf16[1,32,2816]{2,1,0:T(8,128)(2,1)S(1)}, u32[]{:S(2)}, u32[]{:S(2)}) collective-permute-start(bf16[1,32,2816]{2,1,0:T(8,128)(2,1)} %get-tuple-element.232), channel_id=1, source_target_pairs={{0,2},{2,0},{4,6},{6,4},{1,3},{3,1},{5,7},{7,5},{8,10},{10,8},{12,... | collective-permute-start | bytes 540680 | tf_op jit(solution)/shard_map/ppermute | solution.py:376
  620.9 13.8 %collective-permute-start.50 = (bf16[64,1536]{1,0:T(8,128)(2,1)S(1)}, bf16[64,1536]{1,0:T(8,128)(2,1)S(1)}, u32[]{:S(2)}, u32[]{:S(2)}) collective-permute-start(bf16[64,1536]{1,0:T(8,128)(2,1)S(1)} %get-tuple-element.193), channel_id=1, source_target_pairs={{0,16},{8,24},{16,0},{24,8},{1,17},{9,25},{17,1},{25,9},{2,18},{10... | collective-permute-start | bytes 589832 | tf_op jit(solution)/shard_map/ppermute | solution.py:457
  624.7 10.0 %collective-permute-start.49 = (bf16[64,1536]{1,0:T(8,128)(2,1)S(1)}, bf16[64,1536]{1,0:T(8,128)(2,1)S(1)}, u32[]{:S(2)}, u32[]{:S(2)}) collective-permute-start(bf16[64,1536]{1,0:T(8,128)(2,1)S(1)} %get-tuple-element.192), channel_id=1, source_target_pairs={{0,8},{8,16},{16,24},{24,0},{1,9},{9,17},{17,25},{25,1},{2,10},{10... | collective-permute-start | bytes 589832 | tf_op jit(solution)/shard_map/ppermute | solution.py:457
  (104 other events, 1119.2 us)
Sparse Core Ops, SparseCore 0:
  175.6 33.0 all-gather.5

commit v2 on v1

--- a/solution.py
+++ b/solution.py
@@ -409,12 +409,17 @@
     return jnp.concatenate([x_first(array[:half]), y_first(array[half:])], axis=0)
 
 
-def gather_rows(shard):
+def after(array, done):
+    return array if done is None else lax.optimization_barrier((array, done))[0]
+
+
+def gather_rows(shard, done=None):
     rows, columns = shard.shape
     count, ctx = lax.axis_size("fsdp"), lax.axis_size("ctx")
     if ctx != 4 or count % 2:
-        return lax.all_gather(shard, "fsdp", axis=0, tiled=True)
+        return lax.all_gather(shard, "fsdp", axis=0, tiled=True), None
     part = lax.dynamic_slice_in_dim(shard, lax.axis_index("ctx") * (rows // ctx), rows // ctx, 0)
+    part = after(part, done)
     if count > 4:
         pieces = lax.all_gather(part, "fsdp", axis=0)
     else:
@@ -424,10 +429,10 @@
         for shift in range(1, count):
             moved = lax.ppermute(part, "fsdp", [(i, (i + shift) % count) for i in range(count)])
             pieces = lax.dynamic_update_index_in_dim(pieces, moved, (place - shift) % count, 0)
-    return along_ctx(pieces).reshape(count * rows, columns)
-
-
-def reduce_rows(grad):
+    return along_ctx(pieces).reshape(count * rows, columns), pieces
+
+
+def reduce_rows(grad, done=(None, None)):
     rows, columns = grad.shape
     count, ctx = lax.axis_size("fsdp"), lax.axis_size("ctx")
     grad = grad.astype(BF)
@@ -440,12 +445,12 @@
     blocks = grad.reshape(count, 2, 2, size, columns)
     half = count // 2
 
-    def fold(array, bit, step, axis):
-        theirs = swap(pick(array, 1 - bit, axis), "ctx", step)
+    def fold(array, bit, step, axis, late):
+        theirs = after(swap(pick(array, 1 - bit, axis), "ctx", step), late)
         return (pick(array, bit, axis).astype(F32) + theirs.astype(F32)).astype(BF)
 
-    first = fold(fold(blocks[:half], x_bit, 1, 2), y_bit, 2, 1)
-    second = fold(fold(blocks[half:], y_bit, 2, 1), x_bit, 1, 1)
+    first = fold(fold(blocks[:half], x_bit, 1, 2, done[0]), y_bit, 2, 1, done[1])
+    second = fold(fold(blocks[half:], y_bit, 2, 1, done[0]), x_bit, 1, 1, done[1])
     partial = jnp.concatenate([first, second], axis=0)
     if count > 4:
         own = lax.psum_scatter(partial, "fsdp", scatter_dimension=0, tiled=False)
@@ -485,11 +490,28 @@
     )
 
 
-def chain(decay, state, order, used):
-    out = jnp.zeros_like(state[0])
-    for source in order:
-        out = jnp.where(used(source), decay[source] * out + state[source].astype(F32), out)
+def carried(decay, state, step):
+    heads = state.shape[0] // VH
+    packed = jnp.concatenate([state, decay.reshape(heads, KH)], axis=0).astype(BF)
+    out = jnp.zeros_like(state)
+    moved = [shifted(packed, "ctx", step * far) for far in range(1, lax.axis_size("ctx"))]
+    for piece in reversed(moved):
+        piece = piece.astype(F32)
+        grown = jnp.repeat(piece[heads * VH :], VH, axis=0)
+        out = grown * out + piece[: heads * VH]
     return out
+
+
+def sum_all(array):
+    for axis in ("ctx", "fsdp"):
+        count, bit = lax.axis_size(axis), 1
+        if count & (count - 1):
+            array = lax.psum(array, axis)
+            continue
+        while bit < count:
+            array = array + swap(array, axis, bit)
+            bit *= 2
+    return array
 
 
 def body(
@@ -521,16 +543,17 @@
         [w_query, w_key, w_value, w_outgate, w_lowrank, prenorm[:, None], postnorm[:, None], pad],
         axis=1,
     )
-    mixer_all = gather_rows(mixer_pack)
-    mat_output = gather_rows(w_output.T).T
-    mat_ffn = gather_rows(jnp.concatenate([w_gate, w_up], axis=1))
-    mat_down_t = gather_rows(w_down.T)
+    mixer_all, pieces = gather_rows(mixer_pack)
+    ffn_pack = jnp.concatenate([w_gate, w_up, w_down.T, w_output.T], axis=1)
+    ffn_all, _ = gather_rows(ffn_pack, pieces)
+    mat_ffn = ffn_all[:, : 2 * hidden_size]
+    mat_down_t = ffn_all[:, 2 * hidden_size : 3 * hidden_size]
+    mat_output_t = ffn_all[:, 3 * hidden_size :]
     mat_lowrank = mixer_all[:, mixer_size : mixer_size + rank]
     gain_first = mixer_all[:, mixer_size + rank].astype(F32)
     gain_second = mixer_all[:, mixer_size + rank + 1].astype(F32)
     gain_head = headnorm.astype(F32)[None, :]
 
-    place, pieces = lax.axis_index("ctx"), lax.axis_size("ctx")
     ids = doc_ids[0]
     last_id = ids[-1:]
     prev_id = shifted(last_id, "ctx", 1)
@@ -551,16 +574,12 @@
 
     total, ending, decay_sum = ending_call(ids, prev_id, ids_col, key, value, log_decay)
     through = jnp.exp(decay_sum) * link
-    through_all = lax.all_gather(through, "ctx")
-    ending_all = lax.all_gather(ending, "ctx")
-    columns = jnp.repeat(through_all.reshape(pieces, heads, 1, KH), VH, axis=2)
-    columns = columns.reshape(pieces, heads * VH, KH)
-    incoming = chain(columns, ending_all, range(pieces), lambda source: source < place)
+    incoming = carried(through, ending, 1)
     mixed, gated, states = forward_call(
         ids, prev_id, ids_col, ids_row, query, key, value, total, gate_pre, gain_head, incoming
     )
 
-    resid_mid = resid_in + both(dot(gated, mat_output))
+    resid_mid = resid_in + both(dot(gated, mat_output_t, 1, 1))
     scale_two = rms_scale(resid_mid)
     normed_two = (resid_mid * scale_two * gain_second).astype(BF)
     acts = dot(normed_two, mat_ffn)
@@ -575,21 +594,19 @@
     grad_up_act = (grad_hidden * silu_act).astype(BF)
     grad_acts = jnp.concatenate([grad_gate_act, grad_up_act], axis=1)
     norm_two_grad = both(dot(grad_acts, mat_ffn, 1, 1))
-    grad_down = reduce_rows(dot(cot, hidden, 0, 0).astype(BF)).T
-    grad_ffn = reduce_rows(dot(normed_two, grad_acts, 0, 0).astype(BF))
+    grad_wide = jnp.concatenate(
+        [dot(normed_two, grad_acts, 0, 0).astype(BF), dot(cot, hidden, 0, 0).astype(BF)], axis=1
+    )
+    grad_wide = after(grad_wide, norm_two_grad)
     grad_postnorm = jnp.sum(norm_two_grad * resid_mid * scale_two, axis=0)
     grad_mid = cot.astype(F32) + norm_back(norm_two_grad, resid_mid, scale_two, gain_second)
     grad_attn = grad_mid.astype(BF)
-    grad_gated = dot(grad_attn, mat_output, 1, 1)
-    grad_output = reduce_rows(dot(grad_attn, gated, 0, 0).astype(BF)).T
+    grad_gated = dot(grad_attn, mat_output_t)
 
     grad_mixed, grad_gate_rows, headnorm_part, adjoint = back_start_call(
         ids, prev_id, ids_col, query, total, gate_pre, gain_head, mixed, grad_gated
     )
-    adjoint_all = lax.all_gather(adjoint.astype(BF), "ctx")
-    adjoint_in = chain(
-        columns, adjoint_all, range(pieces - 1, -1, -1), lambda source: source > place
-    )
+    adjoint_in = carried(through, adjoint, -1)
     grad_query, grad_key, grad_value, grad_log_decay = backward_call(
         ids, prev_id, ids_col, ids_row, query, key, value, total, grad_mixed, states, adjoint_in
     )
@@ -598,43 +615,41 @@
     grad_bias = jnp.sum(grad_logit.astype(F32), axis=0, keepdims=True)
     grad_rank = both(dot(grad_logit, w_decay, 1, 1)).astype(BF)
     grad_heads = jnp.concatenate([grad_query, grad_key, grad_value, grad_gate_rows], axis=1)
-    grad_mixer = dot(normed_one, grad_heads, 0, 0).astype(BF)
-    grad_lowrank = dot(normed_one, grad_rank, 0, 0).astype(BF)
+    grad_mixer = jnp.concatenate(
+        [dot(normed_one, grad_heads, 0, 0).astype(BF), dot(grad_attn, gated, 0, 0).astype(BF)],
+        axis=1,
+    )
+    grad_lowrank = dot(grad_rank, normed_one, 0, 0)
     norm_one_grad = both(dot(grad_heads, mixer_all[:, :mixer_size], 1, 1))
     norm_one_grad = norm_one_grad + dot(grad_rank, mat_lowrank, 1, 1)
     grad_prenorm = jnp.sum(norm_one_grad * resid_in * scale_one, axis=0)
     grad_tokens = (grad_mid + norm_back(norm_one_grad, resid_in, scale_one, gain_first)).astype(BF)
-    grad_heads_own = reduce_rows(grad_mixer)
-    grad_small = jnp.concatenate(
-        [
-            grad_lowrank,
-            grad_prenorm[:, None].astype(BF),
-            grad_postnorm[:, None].astype(BF),
-            jnp.zeros((grad_lowrank.shape[0], extra), BF),
-        ],
-        axis=1,
-    )
-    small_own = reduce_rows(grad_small)
-    sums = lax.psum(
-        jnp.concatenate([grad_decay, grad_bias, both(headnorm_part)], axis=0), ("fsdp", "ctx")
-    )
+    wide_own = reduce_rows(grad_wide, (grad_mixed, grad_query))
+    heads_own = reduce_rows(grad_mixer)
+    width = tokens.shape[2]
+    tall = jnp.concatenate([grad_lowrank, grad_prenorm[None], grad_postnorm[None]], axis=0)
+    narrow = jnp.concatenate([grad_decay, grad_bias, both(headnorm_part)], axis=0)
+    sums = sum_all(jnp.concatenate([tall, narrow], axis=1))
+    rows = prenorm.shape[0]
+    small_own = lax.dynamic_slice_in_dim(sums, lax.axis_index("fsdp") * rows, rows, 1)
+    narrow = sums[:, width:]
     return (
         block_out[None],
         grad_tokens[None],
-        small_own[:, rank],
-        grad_heads_own[:, :keys],
-        grad_heads_own[:, keys : 2 * keys],
-        grad_heads_own[:, 2 * keys : 2 * keys + values],
-        grad_heads_own[:, 2 * keys + values :],
-        small_own[:, :rank],
-        sums[:rank],
-        sums[rank],
-        sums[rank + 1],
-        grad_output,
-        small_own[:, rank + 1],
-        grad_ffn[:, :hidden_size],
-        grad_ffn[:, hidden_size:],
-        grad_down,
+        small_own[rank],
+        heads_own[:, :keys],
+        heads_own[:, keys : 2 * keys],
+        heads_own[:, 2 * keys : 2 * keys + values],
+        heads_own[:, 2 * keys + values : mixer_size],
+        small_own[:rank].T,
+        narrow[:rank],
+        narrow[rank],
+        narrow[rank + 1],
+        heads_own[:, mixer_size:].T,
+        small_own[rank + 1],
+        wide_own[:, :hidden_size],
+        wide_own[:, hidden_size : 2 * hidden_size],
+        wide_own[:, 2 * hidden_size :].T,
     )
 
 

time: 697 us -> 486 us (0.70)
  blocking collectives: 94.5 us -> 0 us
  waiting for transfers between devices: 214 us -> 152 us
  local copies, waits for them, and re-layouts: 80.2 us -> 57 us
  starting transfers between devices: 113 us -> 91.7 us
  between operations: 17.4 us -> 3.68 us
    ppermute x62 -> x34, waiting for transfers between devices: 160 us -> 80.5 us  [swap(): return lax.ppermute(array, axis, [(i, i ^ bit) for i in range(count)])]
    psum x1 -> x0, blocking collectives: 76.9 us -> none  [body(): lax.psum(jnp.concatenate([grad_decay, grad_bias, both(headnorm_part)], ax...]
    ppermute x62 -> x34, starting transfers between devices: 62.2 us -> 36.8 us  [swap(): return lax.ppermute(array, axis, [(i, i ^ bit) for i in range(count)])]
    all_gather x2 -> x0, blocking collectives: 17.6 us -> none  [the longest x1 9.1 us: body(): adjoint_all = lax.all_gather(adjoint.astype(BF), 'ctx')]
    ppermute x12 -> x6, starting transfers between devices: 26.5 us -> 10.8 us  [gather_rows(): lax.ppermute(part, 'fsdp', [(i, (i + shift) % count) for i in range(count)])]
    ppermute x15 -> x6, waiting for transfers between devices: 30.1 us -> 45 us  [reduce_rows(): lax.ppermute(sent, 'fsdp', [(i, (i + shift) % count) for i in range(count)])]
    ppermute x12 -> x6, waiting for transfers between devices: 9.04 us -> 23.8 us  [gather_rows(): lax.ppermute(part, 'fsdp', [(i, (i + shift) % count) for i in range(count)])]
    all_gather x1 -> x0, waiting for transfers between devices: 14.7 us -> none  [body(): ending_all = lax.all_gather(ending, 'ctx')]
  transfers between devices with their start and end apart: 91 -> 53, of which waited for: 49 -> 19; matrix products, arithmetic and copies ran while one was open for 21% -> 23% of each run, Pallas kernels for 6% -> 8%
where the time goes in v2:
time: 486 us; the launch traced here: 477 us
  waiting for transfers between devices  152 us (31%)
  starting transfers between devices  91.7 us (19%)
  matrix products  79.2 us (16%)
  local copies, waits for them, and re-layouts  57 us (12%)
  other arithmetic  52.5 us (11%)
  Pallas kernels  40.2 us (8%)
    ppermute x34, waiting for transfers between devices, swap(): return lax.ppermute(array, axis, [(i, i ^ bit) for i in range(count)])  80.5 us
    dot_general x17, matrix products, dot(): lax.dot_general(left, right, (((left_dim,), (right_dim,)), ((), ())), pre...  79.2 us
    ppermute x6, waiting for transfers between devices, reduce_rows(): lax.ppermute(sent, 'fsdp', [(i, (i + shift) % count) for i in range(count)])  45 us
    pallas_call x4, Pallas kernels, call(): pl.pallas_call(kernel, out_shape=shapes, in_specs=[pl.BlockSpec(memory_sp...  40.2 us
    ppermute x34, starting transfers between devices, swap(): return lax.ppermute(array, axis, [(i, i ^ bit) for i in range(count)])  36.8 us
    ppermute x6, starting transfers between devices, reduce_rows(): lax.ppermute(sent, 'fsdp', [(i, (i + shift) % count) for i in range(count)])  29.8 us
    unnamed x95, local copies, waits for them, and re-layouts  29 us
    ppermute x6, waiting for transfers between devices, gather_rows(): lax.ppermute(part, 'fsdp', [(i, (i + shift) % count) for i in range(count)])  23.8 us
  transfers between devices with their start and end apart: 53, of which 19 were waited for; matrix products, arithmetic and copies ran while one was open for 23% of the time, Pallas kernels for 8%

profile of v2, /device:TPU:0, one launch (start us, length us, event | category | flops | bytes accessed | tf_op | source)
XLA Modules:
  0.0 476.6 jit_solution(1609184441607966373)
XLA Ops:
  5.2 3.0 collective-permute-start.1
  8.2 2.6 collective-permute-start.2
  12.7 4.0 collective-permute-start
  17.0 2.9 copy.59
  20.4 2.5 copy.68
  31.2 2.6 collective-permute-start.12
  37.0 7.8 %collective-permute-done.4 = bf16[2,64,1664]{2,1,0:T(8,128)(2,1)S(1)} collective-permute-done((bf16[2,64,1664]{2,1,0:T(8,128)(2,1)S(1)}, bf16[2,64,1664]{2,1,0:T(8,128)(2,1)S(1)}, u32[]{:S(2)}, u32[]{:S(2)}) %collective-permute-start.4) | collective-permute-done | bytes 426016 | tf_op jit(solution)/shard_map/ppermute | solution.py:376
  48.8 23.6 %collective-permute-done.12 = bf16[64,4736]{1,0:T(8,128)(2,1)S(1)} collective-permute-done((bf16[64,4736]{1,0:T(8,128)(2,1)S(1)}, bf16[64,4736]{1,0:T(8,128)(2,1)S(1)}, u32[]{:S(2)}, u32[]{:S(2)}) %collective-permute-start.12) | collective-permute-done | bytes 606240 | tf_op jit(solution)/shard_map/ppermute | solution.py:430
  78.6 6.4 %fusion.119 = (bf16[1024,1664]{1,0:T(8,128)(2,1)S(1)}, f32[1024,1664]{1,0:T(8,128)}) fusion(bf16[1024,1664]{1,0:T(8,128)(2,1)S(1)} %bitcast.352, bf16[1,1024,1024]{1,2,0:T(8,128)(2,1)S(1)} %copy.59, f32[1024]{0:T(1024)S(1)} %get-tuple-element.93, f32[1024]{0:T(1024)S(1)} %add_rsqrt_fusion.1), kind=kOutput, calls=%fused_computation.278 | convolution fusion | flops 3495559168 | bytes 15736832 | tf_op jit(solution)/shard_map/dot_general | solution.py:477
  85.2 2.6 fusion.64
  87.8 5.8 %shard_map.288 = (f32[1024,256]{1,0:T(8,128)S(1)}, f32[512,128]{1,0:T(8,128)S(1)}, f32[1,256]{1,0:T(1,128)S(1)}) custom-call(s32[1024]{0:T(1024)S(1)} %bitcast.328, s32[1]{0:T(128)} %collective-permute-done.prev_s, s32[1024,1]{1,0:T(8,128)S(1)} %copy.67.ids_c, bf16[1024,256]{1,0:T(8,128)(2,1)S(1)} %get-tuple-element.124.key, ...), custom_call_target="tpu_custom_call" | custom-call | flops 8000000000 | bytes 3941380 | tf_op jit(solution)/shard_map/pallas_call | solution.py:299
  94.6 2.4 collective-permute-start.9
  97.0 2.7 collective-permute-start.8
  102.3 3.2 slice.263.gate
  105.5 3.1 collective-permute-done.9
  112.9 2.5 collective-permute-start.15
  116.3 9.0 %shard_map.289 = (f32[1024,512]{1,0:T(8,128)}, bf16[1024,512]{1,0:T(8,128)(2,1)S(1)}, bf16[16,512,128]{2,1,0:T(8,128)(2,1)}) custom-call(s32[1024]{0:T(1024)S(1)} %bitcast.329, s32[1]{0:T(128)} %collective-permute-done.prev_s, s32[1024,1]{1,0:T(8,128)S(1)} %copy.67.ids_c, s32[16,64]{1,0:T(8,128)S(1)} %reshape_squeeze.3.ids_r, ...), custom_call_target="tpu_custom_call" | custom-call | flops 20000000000 | bytes 10761220 | tf_op jit(solution)/shard_map/pallas_call | solution.py:299
  125.3 42.0 %collective-permute-done.15 = bf16[2,2,64,4736]{3,2,0,1:T(8,128)(2,1)} collective-permute-done((bf16[2,2,64,4736]{3,2,0,1:T(8,128)(2,1)}, bf16[2,2,64,4736]{3,2,0,1:T(8,128)(2,1)}, u32[]{:S(2)}, u32[]{:S(2)}) %collective-permute-start.15) | collective-permute-done | bytes 2424864 | tf_op jit(solution)/shard_map/ppermute | solution.py:376
  175.5 3.1 convolution_convert_fusion.3
  179.8 4.0 copy.74
  184.3 4.6 multiply_reduce_fusion.2
  189.4 9.4 %fusion.12 = f32[1024,2816]{1,0:T(8,128)} fusion(bf16[1024,4736]{1,0:T(8,128)(2,1)S(1)} %bitcast.341, f32[1024,1024]{0,1:T(8,128)S(1)} %get-tuple-element.97, f32[1024]{0:T(1024)S(1)} %get-tuple-element.92, f32[1024]{0:T(1024)S(1)} %add_rsqrt_fusion), kind=kOutput, calls=%fused_computation.22 | convolution fusion | flops 5908725760 | bytes 21504000 | tf_op jit(solution)/shard_map/dot_general | solution.py:477
  198.8 9.6 %fusion.2 = (bf16[1024,1408]{1,0:T(8,128)(2,1)}, bf16[1024,1408]{1,0:T(8,128)(2,1)}, bf16[1024,1408]{1,0:T(8,128)(2,1)S(1)}) fusion(f32[1024,2816]{1,0:T(8,128)} %fusion.12, bf16[1024,4736]{1,0:T(8,128)(2,1)S(1)} %bitcast.342, bf16[1,1024,1024]{2,1,0:T(8,128)(2,1)S(1)} %copy-done.25), kind=kOutput, calls=%fused_computation.7 | convolution fusion | flops 2974416896 | bytes 25165824 | tf_op jit(solution)/shard_map/dot_general | solution.py:477
  210.0 5.0 %fusion.54 = bf16[1024,1024]{0,1:T(8,128)(2,1)} fusion(bf16[1024,1408]{1,0:T(8,128)(2,1)S(1)} %get-tuple-element.102, bf16[1024,4736]{1,0:T(8,128)(2,1)S(1)} %bitcast.343), kind=kOutput, calls=%fused_computation.108 | convolution fusion | flops 2953838592 | bytes 7864320 | tf_op jit(solution)/shard_map/dot_general | solution.py:477
  215.0 5.5 %fusion.30 = bf16[1024,1408]{1,0:T(8,128)(2,1)S(1)} fusion(bf16[1024,1408]{1,0:T(8,128)(2,1)} %copy-done.40, bf16[1,1024,1024]{2,1,0:T(8,128)(2,1)S(1)} %copy-done.25), kind=kOutput, calls=%fused_computation.58 | convolution fusion | flops 2954231808 | bytes 7864320 | tf_op jit(solution)/shard_map/dot_general | solution.py:477
  220.6 8.2 %fusion.51 = bf16[1024,1024]{0,1:T(8,128)(2,1)S(1)} fusion(bf16[1024,4736]{1,0:T(8,128)(2,1)S(1)} %bitcast.344, bf16[1024,1408]{1,0:T(8,128)(2,1)} %get-tuple-element.101, bf16[1024,1408]{1,0:T(8,128)(2,1)} %get-tuple-element.100), kind=kOutput, calls=%fused_computation.107 | convolution fusion | flops 5918162944 | bytes 13631488 | tf_op jit(solution)/shard_map/dot_general | solution.py:477
  228.7 10.9 %convolution_convert_fusion = bf16[1024,2816]{1,0:T(8,128)(2,1)} fusion(bf16[1024,1408]{1,0:T(8,128)(2,1)} %get-tuple-element.101, bf16[1024,1408]{1,0:T(8,128)(2,1)} %get-tuple-element.100, f32[1024,1024]{0,1:T(8,128)S(1)} %get-tuple-element.97, f32[1024]{0:T(1024)S(1)} %get-tuple-element.92, f32[1024]{0:T(1024)S(1)} %add_rsqrt_fusion), kind=kOutput, calls=%fused_computation.12 | convolution fusion | flops 5923143680 | bytes 15736832 | tf_op jit(solution)/shard_map/dot_general | solution.py:477
  240.2 3.6 pad_maximum_fusion.1
  254.5 5.5 %multiply_add_fusion = (f32[1024,1024]{0,1:T(8,128)S(1)}, bf16[1,1024,1024]{1,2,0:T(8,128)(2,1)}) fusion(f32[1024,1024]{0,1:T(8,128)S(1)} %get-tuple-element.97, bf16[1,1024,1024]{1,2,0:T(8,128)(2,1)S(1)} %copy-done.20, f32[1024]{0:T(1024)S(1)} %broadcast_multiply_fusion.1, f32[1024]{0:T(1024)S(1)} %get-tuple-element.92, f32[1024]{0:T(1024)S(1)} %add_rsqrt_fusion, ...), kind=kLoop, calls=%fused_computation.49 | loop fusion | flops 16777216 | bytes 20983808 | tf_op jit(solution)/shard_map/add | solution.py:602
  260.0 4.7 fusion.68.grad_gated
  264.7 7.8 %shard_map.290 = (bf16[1024,512]{1,0:T(8,128)(2,1)S(1)}, bf16[1024,512]{1,0:T(8,128)(2,1)S(1)}, f32[1,256]{1,0:T(1,128)S(1)}, f32[512,128]{1,0:T(8,128)S(1)}) custom-call(s32[1024]{0:T(1024)S(1)} %bitcast.330, s32[1]{0:T(128)} %collective-permute-done.prev_s, s32[1024,1]{1,0:T(8,128)S(1)} %copy.67.ids_c, bf16[1024,256]{1,0:T(8,128)(2,1)S(1)} %get-tuple-element.125.query, ...), custom_call_target="tpu_custom_call" | custom-call | flops 15000000512 | bytes 10233860 | tf_op jit(solution)/shard_map/pallas_call | solution.py:299
  277.5 3.9 copy.95
  282.7 15.0 %collective-permute-done.42 = bf16[2,2,64,4224]{3,2,0,1:T(8,128)(2,1)} collective-permute-done((bf16[2,2,64,4224]{3,2,0,1:T(8,128)(2,1)}, bf16[2,2,64,4224]{3,2,0,1:T(8,128)(2,1)}, u32[]{:S(2)}, u32[]{:S(2)}) %collective-permute-start.42) | collective-permute-done | bytes 2162720 | tf_op jit(solution)/shard_map/ppermute | solution.py:376
  297.7 3.0 fusion.17
  302.5 2.3 fusion.16
  305.9 3.2 collective-permute-start.45
  309.3 17.7 %shard_map.291 = (bf16[1024,256]{1,0:T(8,128)(2,1)S(1)}, bf16[1024,256]{1,0:T(8,128)(2,1)S(1)}, bf16[1024,512]{1,0:T(8,128)(2,1)S(1)}, f32[1024,256]{1,0:T(8,128)}) custom-call(s32[1024]{0:T(1024)S(1)} %bitcast.331, s32[1]{0:T(128)} %collective-permute-done.prev_s, s32[1024,1]{1,0:T(8,128)S(1)} %copy.67.ids_c, s32[16,64]{1,0:T(8,128)S(1)} %reshape_squeeze.3.ids_r, ...), custom_call_target="tpu_custom_call" | custom-call | flops 40000000000 | bytes 9711620 | tf_op jit(solution)/shard_map/pallas_call | solution.py:299
  329.0 3.7 fusion.57
  332.8 3.9 convolution_convert_fusion.2
  345.3 13.5 %collective-permute-start.48 = (bf16[64,4224]{1,0:T(8,128)(2,1)S(1)}, bf16[64,4224]{1,0:T(8,128)(2,1)S(1)}, u32[]{:S(2)}, u32[]{:S(2)}) collective-permute-start(bf16[64,4224]{1,0:T(8,128)(2,1)S(1)} %get-tuple-element.132), channel_id=1, source_target_pairs={{0,24},{8,0},{16,8},{24,16},{1,25},{9,1},{17,9},{25,17},{2,26},{10... | collective-permute-start | bytes 1622024 | tf_op jit(solution)/shard_map/ppermute | solution.py:462
  360.4 3.7 collective-permute-done.31
  364.1 13.6 %collective-permute-start.46 = (bf16[64,4224]{1,0:T(8,128)(2,1)S(1)}, bf16[64,4224]{1,0:T(8,128)(2,1)S(1)}, u32[]{:S(2)}, u32[]{:S(2)}) collective-permute-start(bf16[64,4224]{1,0:T(8,128)(2,1)S(1)} %get-tuple-element.130), channel_id=1, source_target_pairs={{0,8},{8,16},{16,24},{24,0},{1,9},{9,17},{17,25},{25,1},{2,10},{10... | collective-permute-start | bytes 1622024 | tf_op jit(solution)/shard_map/ppermute | solution.py:462
  379.0 28.3 %collective-permute-done.47 = bf16[64,4224]{1,0:T(8,128)(2,1)S(1)} collective-permute-done((bf16[64,4224]{1,0:T(8,128)(2,1)S(1)}, bf16[64,4224]{1,0:T(8,128)(2,1)S(1)}, u32[]{:S(2)}, u32[]{:S(2)}) %collective-permute-start.47) | collective-permute-done | bytes 540704 | tf_op jit(solution)/shard_map/ppermute | solution.py:462
  412.8 2.6 collective-permute-done.49
  419.5 15.4 %collective-permute-done.36 = bf16[64,2048]{1,0:T(8,128)(2,1)S(1)} collective-permute-done((bf16[64,2048]{1,0:T(8,128)(2,1)S(1)}, bf16[64,2048]{1,0:T(8,128)(2,1)S(1)}, u32[]{:S(2)}, u32[]{:S(2)}) %collective-permute-start.36) | collective-permute-done | bytes 262176 | tf_op jit(solution)/shard_map/ppermute | solution.py:462
  448.9 2.6 copy.96
  455.2 2.3 collective-permute-done.39
  466.9 4.8 %collective-permute-start.30 = (f32[18,1280]{1,0:T(8,128)S(1)}, f32[18,1280]{1,0:T(8,128)S(1)}, u32[]{:S(2)}, u32[]{:S(2)}) collective-permute-start(f32[18,1280]{1,0:T(8,128)S(1)} %add.301), channel_id=1, source_target_pairs={{0,16},{8,24},{16,0},{24,8},{1,17},{9,25},{17,1},{25,9},{2,18},{10... | collective-permute-start | bytes 276488 | tf_op jit(solution)/shard_map/ppermute | solution.py:376
  (308 shorter events, 123.2 us)
Async XLA Ops:
  5.2 22.0 %collective-permute-start.1 = (bf16[64,1664]{1,0:T(8,128)(2,1)}, bf16[64,1664]{1,0:T(8,128)(2,1)}, u32[]{:S(2)}, u32[]{:S(2)}) collective-permute-start(bf16[64,1664]{1,0:T(8,128)(2,1)} %get-tuple-element.99), channel_id=1, source_target_pairs={{0,8},{8,16},{16,24},{24,0},{1,9},{9,17},{17,25},{25,1},{2,10},{10... | collective-permute-start | bytes 638984 | tf_op jit(solution)/shard_map/ppermute | solution.py:430
  8.2 19.9 %collective-permute-start.2 = (bf16[64,1664]{1,0:T(8,128)(2,1)}, bf16[64,1664]{1,0:T(8,128)(2,1)}, u32[]{:S(2)}, u32[]{:S(2)}) collective-permute-start(bf16[64,1664]{1,0:T(8,128)(2,1)} %get-tuple-element.99), channel_id=1, source_target_pairs={{0,16},{8,24},{16,0},{24,8},{1,17},{9,25},{17,1},{25,9},{2,18},{10... | collective-permute-start | bytes 638984 | tf_op jit(solution)/shard_map/ppermute | solution.py:430
  10.8 18.3 %collective-permute-start.3 = (bf16[64,1664]{1,0:T(8,128)(2,1)}, bf16[64,1664]{1,0:T(8,128)(2,1)}, u32[]{:S(2)}, u32[]{:S(2)}) collective-permute-start(bf16[64,1664]{1,0:T(8,128)(2,1)} %get-tuple-element.99), channel_id=1, source_target_pairs={{0,24},{8,0},{16,8},{24,16},{1,25},{9,1},{17,9},{25,17},{2,26},{10... | collective-permute-start | bytes 638984 | tf_op jit(solution)/shard_map/ppermute | solution.py:430
  12.7 13.1 %collective-permute-start = (s32[1]{0:T(128)}, s32[1]{0:T(128)}, u32[]{:S(2)}, u32[]{:S(2)}) collective-permute-start(s32[1]{0:T(128)} %bitcast.2), channel_id=1, source_target_pairs={{0,2},{2,4},{4,6},{1,3},{3,5},{5,7},{8,10},{10,12},{12,14},{9,11},... | collective-permute-start | bytes 20 | tf_op jit(solution)/shard_map/ppermute | solution.py:473
  30.1 18.6 %collective-permute-start.11 = (bf16[64,4736]{1,0:T(8,128)(2,1)S(1)}, bf16[64,4736]{1,0:T(8,128)(2,1)S(1)}, u32[]{:S(2)}, u32[]{:S(2)}) collective-permute-start(bf16[64,4736]{1,0:T(8,128)(2,1)S(1)} %fusion.74), channel_id=1, source_target_pairs={{0,8},{8,16},{16,24},{24,0},{1,9},{9,17},{17,25},{25,1},{2,10},{10... | collective-permute-start | bytes 1818632 | tf_op jit(solution)/shard_map/ppermute | solution.py:430
  31.2 41.2 %collective-permute-start.12 = (bf16[64,4736]{1,0:T(8,128)(2,1)S(1)}, bf16[64,4736]{1,0:T(8,128)(2,1)S(1)}, u32[]{:S(2)}, u32[]{:S(2)}) collective-permute-start(bf16[64,4736]{1,0:T(8,128)(2,1)S(1)} %fusion.74), channel_id=1, source_target_pairs={{0,16},{8,24},{16,0},{24,8},{1,17},{9,25},{17,1},{25,9},{2,18},{10... | collective-permute-start | bytes 1818632 | tf_op jit(solution)/shard_map/ppermute | solution.py:430
  33.8 38.7 %collective-permute-start.13 = (bf16[64,4736]{1,0:T(8,128)(2,1)S(1)}, bf16[64,4736]{1,0:T(8,128)(2,1)S(1)}, u32[]{:S(2)}, u32[]{:S(2)}) collective-permute-start(bf16[64,4736]{1,0:T(8,128)(2,1)S(1)} %fusion.74), channel_id=1, source_target_pairs={{0,24},{8,0},{16,8},{24,16},{1,25},{9,1},{17,9},{25,17},{2,26},{10... | collective-permute-start | bytes 1818632 | tf_op jit(solution)/shard_map/ppermute | solution.py:430
  34.0 10.8 %collective-permute-start.4 = (bf16[2,64,1664]{2,1,0:T(8,128)(2,1)S(1)}, bf16[2,64,1664]{2,1,0:T(8,128)(2,1)S(1)}, u32[]{:S(2)}, u32[]{:S(2)}) collective-permute-start(bf16[2,64,1664]{2,1,0:T(8,128)(2,1)S(1)} %get-tuple-element.159), channel_id=1, source_target_pairs={{0,2},{2,0},{4,6},{6,4},{1,3},{3,1},{5,7},{7,5},{8,10},{10,8},{12,... | collective-permute-start | bytes 1277960 | tf_op jit(solution)/shard_map/ppermute | solution.py:376
  35.2 10.8 %collective-permute-start.6 = (bf16[2,64,1664]{2,1,0:T(8,128)(2,1)S(1)}, bf16[2,64,1664]{2,1,0:T(8,128)(2,1)S(1)}, u32[]{:S(2)}, u32[]{:S(2)}) collective-permute-start(bf16[2,64,1664]{2,1,0:T(8,128)(2,1)S(1)} %get-tuple-element.160), channel_id=1, source_target_pairs={{0,4},{2,6},{4,0},{6,2},{1,5},{3,7},{5,1},{7,3},{8,12},{10,14},{12... | collective-permute-start | bytes 1277960 | tf_op jit(solution)/shard_map/ppermute | solution.py:376
  46.3 31.2 %collective-permute-start.7 = (bf16[2,2,64,1664]{3,2,1,0:T(8,128)(2,1)S(1)}, bf16[2,2,64,1664]{3,2,1,0:T(8,128)(2,1)S(1)}, u32[]{:S(2)}, u32[]{:S(2)}) collective-permute-start(bf16[2,2,64,1664]{3,2,1,0:T(8,128)(2,1)S(1)} %pad_maximum_fusion.18), channel_id=1, source_target_pairs={{0,2},{2,0},{4,6},{6,4},{1,3},{3,1},{5,7},{7,5},{8,10},{10,8},{12,... | collective-permute-start | bytes 2555912 | tf_op jit(solution)/shard_map/ppermute | solution.py:376
  47.0 30.0 %collective-permute-start.5 = (bf16[2,2,64,1664]{3,2,0,1:T(8,128)(2,1)S(1)}, bf16[2,2,64,1664]{3,2,0,1:T(8,128)(2,1)S(1)}, u32[]{:S(2)}, u32[]{:S(2)}) collective-permute-start(bf16[2,2,64,1664]{3,2,0,1:T(8,128)(2,1)S(1)} %pad_maximum_fusion.17), channel_id=1, source_target_pairs={{0,4},{2,6},{4,0},{6,2},{1,5},{3,7},{5,1},{7,3},{8,12},{10,14},{12... | collective-permute-start | bytes 2555912 | tf_op jit(solution)/shard_map/ppermute | solution.py:376
  74.2 34.6 %collective-permute-start.14 = (bf16[2,64,4736]{2,1,0:T(8,128)(2,1)}, bf16[2,64,4736]{2,1,0:T(8,128)(2,1)}, u32[]{:S(2)}, u32[]{:S(2)}) collective-permute-start(bf16[2,64,4736]{2,1,0:T(8,128)(2,1)} %get-tuple-element.128), channel_id=1, source_target_pairs={{0,2},{2,0},{4,6},{6,4},{1,3},{3,1},{5,7},{7,5},{8,10},{10,8},{12,... | collective-permute-start | bytes 3637256 | tf_op jit(solution)/shard_map/ppermute | solution.py:376
  75.4 33.4 %collective-permute-start.16 = (bf16[2,64,4736]{2,1,0:T(8,128)(2,1)}, bf16[2,64,4736]{2,1,0:T(8,128)(2,1)}, u32[]{:S(2)}, u32[]{:S(2)}) collective-permute-start(bf16[2,64,4736]{2,1,0:T(8,128)(2,1)} %get-tuple-element.129), channel_id=1, source_target_pairs={{0,4},{2,6},{4,0},{6,2},{1,5},{3,7},{5,1},{7,3},{8,12},{10,14},{12... | collective-permute-start | bytes 3637256 | tf_op jit(solution)/shard_map/ppermute | solution.py:376
  94.6 14.0 %collective-permute-start.9 = (bf16[514,128]{1,0:T(8,128)(2,1)S(1)}, bf16[514,128]{1,0:T(8,128)(2,1)S(1)}, u32[]{:S(2)}, u32[]{:S(2)}) collective-permute-start(bf16[514,128]{1,0:T(8,128)(2,1)S(1)} %pad_maximum_fusion.26), channel_id=1, source_target_pairs={{0,4},{2,6},{1,5},{3,7},{8,12},{10,14},{9,13},{11,15},{16,20},{18,... | collective-permute-start | bytes 394760 | tf_op jit(solution)/shard_map/ppermute | solution.py:473
  97.0 11.6 %collective-permute-start.8 = (bf16[514,128]{1,0:T(8,128)(2,1)S(1)}, bf16[514,128]{1,0:T(8,128)(2,1)S(1)}, u32[]{:S(2)}, u32[]{:S(2)}) collective-permute-start(bf16[514,128]{1,0:T(8,128)(2,1)S(1)} %pad_maximum_fusion.26), channel_id=1, source_target_pairs={{0,2},{2,4},{4,6},{1,3},{3,5},{5,7},{8,10},{10,12},{12,14},{9,11},... | collective-permute-start | bytes 394760 | tf_op jit(solution)/shard_map/ppermute | solution.py:473
  99.7 8.9 %collective-permute-start.10 = (bf16[514,128]{1,0:T(8,128)(2,1)S(1)}, bf16[514,128]{1,0:T(8,128)(2,1)S(1)}, u32[]{:S(2)}, u32[]{:S(2)}) collective-permute-start(bf16[514,128]{1,0:T(8,128)(2,1)S(1)} %pad_maximum_fusion.26), channel_id=1, source_target_pairs={{0,6},{1,7},{8,14},{9,15},{16,22},{17,23},{24,30},{25,31}} | collective-permute-start | bytes 394760 | tf_op jit(solution)/shard_map/ppermute | solution.py:473
  112.9 54.4 %collective-permute-start.15 = (bf16[2,2,64,4736]{3,2,0,1:T(8,128)(2,1)}, bf16[2,2,64,4736]{3,2,0,1:T(8,128)(2,1)}, u32[]{:S(2)}, u32[]{:S(2)}) collective-permute-start(bf16[2,2,64,4736]{3,2,0,1:T(8,128)(2,1)} %pad_maximum_fusion.8), channel_id=1, source_target_pairs={{0,4},{2,6},{4,0},{6,2},{1,5},{3,7},{5,1},{7,3},{8,12},{10,14},{12... | collective-permute-start | bytes 7274504 | tf_op jit(solution)/shard_map/ppermute | solution.py:376
  115.7 54.8 %collective-permute-start.17 = (bf16[2,2,64,4736]{3,2,1,0:T(8,128)(2,1)S(1)}, bf16[2,2,64,4736]{3,2,1,0:T(8,128)(2,1)}, u32[]{:S(2)}, u32[]{:S(2)}) collective-permute-start(bf16[2,2,64,4736]{3,2,1,0:T(8,128)(2,1)S(1)} %pad_maximum_fusion.9), channel_id=1, source_target_pairs={{0,2},{2,0},{4,6},{6,4},{1,3},{3,1},{5,7},{7,5},{8,10},{10,8},{12,... | collective-permute-start | bytes 7274504 | tf_op jit(solution)/shard_map/ppermute | solution.py:376
  239.6 13.2 %collective-permute-start.20 = (bf16[1024,1024]{0,1:T(8,128)(2,1)S(1)}, bf16[1024,1024]{0,1:T(8,128)(2,1)S(1)}, u32[]{:S(2)}, u32[]{:S(2)}) collective-permute-start(bf16[1024,1024]{0,1:T(8,128)(2,1)S(1)} %fusion.51), channel_id=1, source_target_pairs={{0,1},{1,0},{2,3},{3,2},{4,5},{5,4},{6,7},{7,6},{8,9},{9,8},{10,11... | collective-permute-start | bytes 6291464 | tf_op jit(solution)/shard_map/ppermute | solution.py:376
  240.1 14.3 %collective-permute-start.19 = (bf16[1024,1024]{0,1:T(8,128)(2,1)}, bf16[1024,1024]{0,1:T(8,128)(2,1)}, u32[]{:S(2)}, u32[]{:S(2)}) collective-permute-start(bf16[1024,1024]{0,1:T(8,128)(2,1)} %fusion.54), channel_id=1, source_target_pairs={{0,1},{1,0},{2,3},{3,2},{4,5},{5,4},{6,7},{7,6},{8,9},{9,8},{10,11... | collective-permute-start | bytes 6291464 | tf_op jit(solution)/shard_map/ppermute | solution.py:376
  247.5 50.1 %collective-permute-start.42 = (bf16[2,2,64,4224]{3,2,0,1:T(8,128)(2,1)}, bf16[2,2,64,4224]{3,2,0,1:T(8,128)(2,1)}, u32[]{:S(2)}, u32[]{:S(2)}) collective-permute-start(bf16[2,2,64,4224]{3,2,0,1:T(8,128)(2,1)} %bitcast.324), channel_id=1, source_target_pairs={{0,2},{2,0},{4,6},{6,4},{1,3},{3,1},{5,7},{7,5},{8,10},{10,8},{12,... | collective-permute-start | bytes 6488072 | tf_op jit(solution)/shard_map/ppermute | solution.py:376
  251.1 51.4 %collective-permute-start.44 = (bf16[2,2,64,4224]{3,2,0,1:T(8,128)(2,1)}, bf16[2,2,64,4224]{3,2,0,1:T(8,128)(2,1)}, u32[]{:S(2)}, u32[]{:S(2)}) collective-permute-start(bf16[2,2,64,4224]{3,2,0,1:T(8,128)(2,1)} %bitcast.323), channel_id=1, source_target_pairs={{0,4},{2,6},{4,0},{6,2},{1,5},{3,7},{5,1},{7,3},{8,12},{10,14},{12... | collective-permute-start | bytes 6488072 | tf_op jit(solution)/shard_map/ppermute | solution.py:376
  272.5 36.7 %collective-permute-start.21 = (bf16[514,128]{1,0:T(8,128)(2,1)S(1)}, bf16[514,128]{1,0:T(8,128)(2,1)S(1)}, u32[]{:S(2)}, u32[]{:S(2)}) collective-permute-start(bf16[514,128]{1,0:T(8,128)(2,1)S(1)} %pad_maximum_fusion.25), channel_id=1, source_target_pairs={{2,0},{4,2},{6,4},{3,1},{5,3},{7,5},{10,8},{12,10},{14,12},{11,9},... | collective-permute-start | bytes 394760 | tf_op jit(solution)/shard_map/ppermute | solution.py:473
  273.8 35.3 %collective-permute-start.22 = (bf16[514,128]{1,0:T(8,128)(2,1)S(1)}, bf16[514,128]{1,0:T(8,128)(2,1)S(1)}, u32[]{:S(2)}, u32[]{:S(2)}) collective-permute-start(bf16[514,128]{1,0:T(8,128)(2,1)S(1)} %pad_maximum_fusion.25), channel_id=1, source_target_pairs={{4,0},{6,2},{5,1},{7,3},{12,8},{14,10},{13,9},{15,11},{20,16},{22,... | collective-permute-start | bytes 394760 | tf_op jit(solution)/shard_map/ppermute | solution.py:473
  275.1 6.3 %collective-permute-start.26 = (bf16[1,256]{1,0:T(2,128)(2,1)S(1)}, bf16[1,256]{1,0:T(2,128)(2,1)S(1)}, u32[]{:S(2)}, u32[]{:S(2)}) collective-permute-start(bf16[1,256]{1,0:T(2,128)(2,1)S(1)} %convert_element_type.361), channel_id=1, source_target_pairs={{0,1},{1,0},{2,3},{3,2},{4,5},{5,4},{6,7},{7,6},{8,9},{9,8},{10,11... | collective-permute-start | bytes 1544 | tf_op jit(solution)/shard_map/ppermute | solution.py:376
  281.4 27.8 %collective-permute-start.23 = (bf16[514,128]{1,0:T(8,128)(2,1)S(1)}, bf16[514,128]{1,0:T(8,128)(2,1)S(1)}, u32[]{:S(2)}, u32[]{:S(2)}) collective-permute-start(bf16[514,128]{1,0:T(8,128)(2,1)S(1)} %pad_maximum_fusion.25), channel_id=1, source_target_pairs={{6,0},{7,1},{14,8},{15,9},{22,16},{23,17},{30,24},{31,25}} | collective-permute-start | bytes 394760 | tf_op jit(solution)/shard_map/ppermute | solution.py:473
  300.7 40.6 %collective-permute-start.43 = (bf16[2,64,4224]{2,1,0:T(8,128)(2,1)S(1)}, bf16[2,64,4224]{2,1,0:T(8,128)(2,1)}, u32[]{:S(2)}, u32[]{:S(2)}) collective-permute-start(bf16[2,64,4224]{2,1,0:T(8,128)(2,1)S(1)} %dynamic-slice_bitcast_fusion.1), channel_id=1, source_target_pairs={{0,4},{2,6},{4,0},{6,2},{1,5},{3,7},{5,1},{7,3},{8,12},{10,14},{12... | collective-permute-start | bytes 3244040 | tf_op jit(solution)/shard_map/ppermute | solution.py:376
  305.9 37.1 %collective-permute-start.45 = (bf16[2,64,4224]{2,1,0:T(8,128)(2,1)}, bf16[2,64,4224]{2,1,0:T(8,128)(2,1)}, u32[]{:S(2)}, u32[]{:S(2)}) collective-permute-start(bf16[2,64,4224]{2,1,0:T(8,128)(2,1)} %dynamic-slice_bitcast_fusion), channel_id=1, source_target_pairs={{0,2},{2,0},{4,6},{6,4},{1,3},{3,1},{5,7},{7,5},{8,10},{10,8},{12,... | collective-permute-start | bytes 3244040 | tf_op jit(solution)/shard_map/ppermute | solution.py:376
  337.4 108.0 %collective-permute-start.24 = (bf16[1024,1024]{0,1:T(8,128)(2,1)S(1)}, bf16[1024,1024]{0,1:T(8,128)(2,1)S(1)}, u32[]{:S(2)}, u32[]{:S(2)}) collective-permute-start(bf16[1024,1024]{0,1:T(8,128)(2,1)S(1)} %fusion.57), channel_id=1, source_target_pairs={{0,1},{1,0},{2,3},{3,2},{4,5},{5,4},{6,7},{7,6},{8,9},{9,8},{10,11... | collective-permute-start | bytes 6291464 | tf_op jit(solution)/shard_map/ppermute | solution.py:376
  338.9 25.1 %collective-permute-start.31 = (bf16[2,2,64,2048]{3,2,0,1:T(8,128)(2,1)S(1)}, bf16[2,2,64,2048]{3,2,0,1:T(8,128)(2,1)S(1)}, u32[]{:S(2)}, u32[]{:S(2)}) collective-permute-start(bf16[2,2,64,2048]{3,2,0,1:T(8,128)(2,1)S(1)} %bitcast.362), channel_id=1, source_target_pairs={{0,2},{2,0},{4,6},{6,4},{1,3},{3,1},{5,7},{7,5},{8,10},{10,8},{12,... | collective-permute-start | bytes 3145736 | tf_op jit(solution)/shard_map/ppermute | solution.py:376
  340.6 37.6 %collective-permute-start.33 = (bf16[2,2,64,2048]{3,2,0,1:T(8,128)(2,1)S(1)}, bf16[2,2,64,2048]{3,2,0,1:T(8,128)(2,1)S(1)}, u32[]{:S(2)}, u32[]{:S(2)}) collective-permute-start(bf16[2,2,64,2048]{3,2,0,1:T(8,128)(2,1)S(1)} %bitcast.361), channel_id=1, source_target_pairs={{0,4},{2,6},{4,0},{6,2},{1,5},{3,7},{5,1},{7,3},{8,12},{10,14},{12... | collective-permute-start | bytes 3145736 | tf_op jit(solution)/shard_map/ppermute | solution.py:376
  345.3 33.4 %collective-permute-start.48 = (bf16[64,4224]{1,0:T(8,128)(2,1)S(1)}, bf16[64,4224]{1,0:T(8,128)(2,1)S(1)}, u32[]{:S(2)}, u32[]{:S(2)}) collective-permute-start(bf16[64,4224]{1,0:T(8,128)(2,1)S(1)} %get-tuple-element.132), channel_id=1, source_target_pairs={{0,24},{8,0},{16,8},{24,16},{1,25},{9,1},{17,9},{25,17},{2,26},{10... | collective-permute-start | bytes 1622024 | tf_op jit(solution)/shard_map/ppermute | solution.py:462
  358.8 48.5 %collective-permute-start.47 = (bf16[64,4224]{1,0:T(8,128)(2,1)S(1)}, bf16[64,4224]{1,0:T(8,128)(2,1)S(1)}, u32[]{:S(2)}, u32[]{:S(2)}) collective-permute-start(bf16[64,4224]{1,0:T(8,128)(2,1)S(1)} %get-tuple-element.131), channel_id=1, source_target_pairs={{0,16},{8,24},{16,0},{24,8},{1,17},{9,25},{17,1},{25,9},{2,18},{10... | collective-permute-start | bytes 1622024 | tf_op jit(solution)/shard_map/ppermute | solution.py:462
  364.1 43.3 %collective-permute-start.46 = (bf16[64,4224]{1,0:T(8,128)(2,1)S(1)}, bf16[64,4224]{1,0:T(8,128)(2,1)S(1)}, u32[]{:S(2)}, u32[]{:S(2)}) collective-permute-start(bf16[64,4224]{1,0:T(8,128)(2,1)S(1)} %get-tuple-element.130), channel_id=1, source_target_pairs={{0,8},{8,16},{16,24},{24,0},{1,9},{9,17},{17,25},{25,1},{2,10},{10... | collective-permute-start | bytes 1622024 | tf_op jit(solution)/shard_map/ppermute | solution.py:462
  378.1 33.2 %collective-permute-start.32 = (bf16[2,64,2048]{2,1,0:T(8,128)(2,1)S(1)}, bf16[2,64,2048]{2,1,0:T(8,128)(2,1)S(1)}, u32[]{:S(2)}, u32[]{:S(2)}) collective-permute-start(bf16[2,64,2048]{2,1,0:T(8,128)(2,1)S(1)} %dynamic-slice_bitcast_fusion.3), channel_id=1, source_target_pairs={{0,4},{2,6},{4,0},{6,2},{1,5},{3,7},{5,1},{7,3},{8,12},{10,14},{12... | collective-permute-start | bytes 1572872 | tf_op jit(solution)/shard_map/ppermute | solution.py:376
  378.7 32.8 %collective-permute-start.34 = (bf16[2,64,2048]{2,1,0:T(8,128)(2,1)S(1)}, bf16[2,64,2048]{2,1,0:T(8,128)(2,1)S(1)}, u32[]{:S(2)}, u32[]{:S(2)}) collective-permute-start(bf16[2,64,2048]{2,1,0:T(8,128)(2,1)S(1)} %dynamic-slice_bitcast_fusion.2), channel_id=1, source_target_pairs={{0,2},{2,0},{4,6},{6,4},{1,3},{3,1},{5,7},{7,5},{8,10},{10,8},{12,... | collective-permute-start | bytes 1572872 | tf_op jit(solution)/shard_map/ppermute | solution.py:376
  407.8 7.6 %collective-permute-start.49 = (bf16[1,32,4224]{2,1,0:T(8,128)(2,1)S(1)}, bf16[1,32,4224]{2,1,0:T(8,128)(2,1)S(1)}, u32[]{:S(2)}, u32[]{:S(2)}) collective-permute-start(bf16[1,32,4224]{2,1,0:T(8,128)(2,1)S(1)} %get-tuple-element.167), channel_id=1, source_target_pairs={{0,2},{2,0},{4,6},{6,4},{1,3},{3,1},{5,7},{7,5},{8,10},{10,8},{12,... | collective-permute-start | bytes 811016 | tf_op jit(solution)/shard_map/ppermute | solution.py:376
  409.6 6.9 %collective-permute-start.51 = (bf16[1,32,4224]{2,1,0:T(8,128)(2,1)S(1)}, bf16[1,32,4224]{2,1,0:T(8,128)(2,1)S(1)}, u32[]{:S(2)}, u32[]{:S(2)}) collective-permute-start(bf16[1,32,4224]{2,1,0:T(8,128)(2,1)S(1)} %get-tuple-element.168), channel_id=1, source_target_pairs={{0,4},{2,6},{4,0},{6,2},{1,5},{3,7},{5,1},{7,3},{8,12},{10,14},{12... | collective-permute-start | bytes 811016 | tf_op jit(solution)/shard_map/ppermute | solution.py:376
  411.9 7.5 %collective-permute-start.37 = (bf16[64,2048]{1,0:T(8,128)(2,1)S(1)}, bf16[64,2048]{1,0:T(8,128)(2,1)S(1)}, u32[]{:S(2)}, u32[]{:S(2)}) collective-permute-start(bf16[64,2048]{1,0:T(8,128)(2,1)S(1)} %get-tuple-element.156), channel_id=1, source_target_pairs={{0,24},{8,0},{16,8},{24,16},{1,25},{9,1},{17,9},{25,17},{2,26},{10... | collective-permute-start | bytes 786440 | tf_op jit(solution)/shard_map/ppermute | solution.py:462
  412.0 22.8 %collective-permute-start.36 = (bf16[64,2048]{1,0:T(8,128)(2,1)S(1)}, bf16[64,2048]{1,0:T(8,128)(2,1)S(1)}, u32[]{:S(2)}, u32[]{:S(2)}) collective-permute-start(bf16[64,2048]{1,0:T(8,128)(2,1)S(1)} %get-tuple-element.155), channel_id=1, source_target_pairs={{0,16},{8,24},{16,0},{24,8},{1,17},{9,25},{17,1},{25,9},{2,18},{10... | collective-permute-start | bytes 786440 | tf_op jit(solution)/shard_map/ppermute | solution.py:462
  415.4 19.4 %collective-permute-start.35 = (bf16[64,2048]{1,0:T(8,128)(2,1)S(1)}, bf16[64,2048]{1,0:T(8,128)(2,1)S(1)}, u32[]{:S(2)}, u32[]{:S(2)}) collective-permute-start(bf16[64,2048]{1,0:T(8,128)(2,1)S(1)} %get-tuple-element.154), channel_id=1, source_target_pairs={{0,8},{8,16},{16,24},{24,0},{1,9},{9,17},{17,25},{25,1},{2,10},{10... | collective-permute-start | bytes 786440 | tf_op jit(solution)/shard_map/ppermute | solution.py:462
  417.5 46.0 %collective-permute-start.52 = (bf16[1,2,32,4224]{3,2,1,0:T(8,128)(2,1)}, bf16[1,2,32,4224]{3,2,1,0:T(8,128)(2,1)}, u32[]{:S(2)}, u32[]{:S(2)}) collective-permute-start(bf16[1,2,32,4224]{3,2,1,0:T(8,128)(2,1)} %pad_maximum_fusion.20), channel_id=1, source_target_pairs={{0,2},{2,0},{4,6},{6,4},{1,3},{3,1},{5,7},{7,5},{8,10},{10,8},{12,... | collective-permute-start | bytes 1622024 | tf_op jit(solution)/shard_map/ppermute | solution.py:376
  435.5 6.4 %collective-permute-start.40 = (bf16[1,32,2048]{2,1,0:T(8,128)(2,1)S(1)}, bf16[1,32,2048]{2,1,0:T(8,128)(2,1)S(1)}, u32[]{:S(2)}, u32[]{:S(2)}) collective-permute-start(bf16[1,32,2048]{2,1,0:T(8,128)(2,1)S(1)} %get-tuple-element.180), channel_id=1, source_target_pairs={{0,4},{2,6},{4,0},{6,2},{1,5},{3,7},{5,1},{7,3},{8,12},{10,14},{12... | collective-permute-start | bytes 393224 | tf_op jit(solution)/shard_map/ppermute | solution.py:376
  436.7 28.2 %collective-permute-start.50 = (bf16[1,2,32,4224]{3,2,1,0:T(8,128)(2,1)}, bf16[1,2,32,4224]{3,2,1,0:T(8,128)(2,1)}, u32[]{:S(2)}, u32[]{:S(2)}) collective-permute-start(bf16[1,2,32,4224]{3,2,1,0:T(8,128)(2,1)} %pad_maximum_fusion.19), channel_id=1, source_target_pairs={{0,4},{2,6},{4,0},{6,2},{1,5},{3,7},{5,1},{7,3},{8,12},{10,14},{12... | collective-permute-start | bytes 1622024 | tf_op jit(solution)/shard_map/ppermute | solution.py:376
  442.8 11.3 %collective-permute-start.41 = (bf16[1,2,32,2048]{3,2,1,0:T(8,128)(2,1)}, bf16[1,2,32,2048]{3,2,1,0:T(8,128)(2,1)}, u32[]{:S(2)}, u32[]{:S(2)}) collective-permute-start(bf16[1,2,32,2048]{3,2,1,0:T(8,128)(2,1)} %pad_maximum_fusion.24), channel_id=1, source_target_pairs={{0,2},{2,0},{4,6},{6,4},{1,3},{3,1},{5,7},{7,5},{8,10},{10,8},{12,... | collective-permute-start | bytes 786440 | tf_op jit(solution)/shard_map/ppermute | solution.py:376
  445.2 12.3 %collective-permute-start.39 = (bf16[1,2,32,2048]{3,2,1,0:T(8,128)(2,1)}, bf16[1,2,32,2048]{3,2,1,0:T(8,128)(2,1)}, u32[]{:S(2)}, u32[]{:S(2)}) collective-permute-start(bf16[1,2,32,2048]{3,2,1,0:T(8,128)(2,1)} %pad_maximum_fusion.23), channel_id=1, source_target_pairs={{0,4},{2,6},{4,0},{6,2},{1,5},{3,7},{5,1},{7,3},{8,12},{10,14},{12... | collective-permute-start | bytes 786440 | tf_op jit(solution)/shard_map/ppermute | solution.py:376
  452.2 9.7 %collective-permute-start.28 = (f32[18,1280]{1,0:T(8,128)S(1)}, f32[18,1280]{1,0:T(8,128)S(1)}, u32[]{:S(2)}, u32[]{:S(2)}) collective-permute-start(f32[18,1280]{1,0:T(8,128)S(1)} %fusion.110), channel_id=1, source_target_pairs={{0,4},{2,6},{4,0},{6,2},{1,5},{3,7},{5,1},{7,3},{8,12},{10,14},{12... | collective-permute-start | bytes 276488 | tf_op jit(solution)/shard_map/ppermute | solution.py:376
  466.9 8.2 %collective-permute-start.30 = (f32[18,1280]{1,0:T(8,128)S(1)}, f32[18,1280]{1,0:T(8,128)S(1)}, u32[]{:S(2)}, u32[]{:S(2)}) collective-permute-start(f32[18,1280]{1,0:T(8,128)S(1)} %add.301), channel_id=1, source_target_pairs={{0,16},{8,24},{16,0},{24,8},{1,17},{9,25},{17,1},{25,9},{2,18},{10... | collective-permute-start | bytes 276488 | tf_op jit(solution)/shard_map/ppermute | solution.py:376
  (46 other events, 509.2 us)
